TPU v7x, 32 devices: a whole 2x2x4 slice. The times are simulated.
32 devices in a mesh: slab: 8 (over y, x, core), sub: 4 (over z).
Axes of the slice: x: 2, y: 2, z: 4, core: 2. Of those that a mesh axis runs over, the one named last changes fastest.
Arguments:
- positions: float32 [3, 32768], P(None, 'slab'), may hold values from 0 to 33, as said below
- velocity: float32 [3, 32768], P(None, 'slab'), may hold values from -6 to 6
- density: float32 [32768], P('slab'), may hold values from 0.1 to 10
- pressure: float32 [32768], P('slab'), may hold values from 0.1 to 10
- counts: int32 [256], P('slab'), may hold values from 8 to 128, as said below
- pair_list: int32 [3, 1280], P(None, ('slab', 'sub')), may hold values from -32 to 255, as said below
Outputs:
- rates: float32 [5, 32768], P(None, 'slab')
Inputs may be any that keep to these rules, and one draw needn't show every extreme that they name: `positions`: particle k of leaf g lies in slab floor(g / 32) along x (x minus that index in [0, 1)), in column g mod 32 along y (likewise), and z in [0, 1). `counts`: at least 8 live particles a leaf; some leaf holds 128. `pair_list`: row 0 is a slot's home leaf, a leaf of this device's part of its slab (columns 8 * i to 8 * i + 7 on the device of index i along sub), or -1 for an empty slot. Row 1 is the other leaf, -1 for an empty slot: the home leaf itself, the leaf of the next column cyclically in the same slab, or a leaf of the next slab cyclically whose column is the home column - 1, + 0 or + 1 plus w, modulo 32; w is 0 for home leaves outside the last slab and one shift common to all pairs headed in the last slab. Row 2 is the image offset along y in units of cell width, 0 for an empty slot and for a pair of a leaf with itself; for a pair into the next slab, minus row 2 modulo 32 equals w. A leaf heads at most 5 pairs, each device holds at most 40 live slots, and some device holds exactly that many.
All inputs are finite; a program needn't handle non-finite values.
Results may differ from a plain program's by a relative error of at most 0.0003.
Values sent between devices are 32-bit elements; how exact they have to be, the bound alone decides.
No kernel may reach another device: no remote copies, remote signals or barrier semaphores. Data moves between devices by JAX's collectives and lax.ppermute only.
A program may use at most 64 MiB of HBM per device.

v0:
```python
import functools
import math

import jax
import jax.numpy as jnp
from jax import lax
from jax.experimental import pallas as pl
from jax.experimental.pallas import tpu as pltpu
from jax.sharding import PartitionSpec as P

LEAF = 128
CAND = 5

GAMMA = 5.0 / 3.0
SUPPORT = 1.5
KERNEL_NORM = 21.0 / (2.0 * math.pi * SUPPORT**3)
MOMENT_REG = 0.05
AREA_FLOOR = 0.0001
AWAY = 64.0
UNROLL = 8
ROWS = 64
ROWS_LOG = 6
COST_LEAF, COST_SLOT, COST_PART = 17, 3, 5
F32 = jnp.float32
BF16 = jnp.bfloat16


def shifted(shard, axis, by):
    peers = lax.axis_size(axis)
    return lax.ppermute(shard, axis, [(i, (i + by) % peers) for i in range(peers)])


def swapped(shard, axis, mask):
    peers = lax.axis_size(axis)
    return lax.ppermute(shard, axis, [(i, i ^ mask) for i in range(peers)])


def reciprocal(value):
    return pl.reciprocal(value, approx=True)


def smoothing_of(dist_sq, scale):
    safe = jnp.maximum(dist_sq, 1e-12)
    radius = safe * lax.rsqrt(safe)
    inside = jnp.maximum(1.0 - radius, 0.0)
    square = inside * inside
    return (square * square) * (scale + (scale * 4.0) * radius)


def split_three(value):
    high = value.astype(BF16).astype(F32)
    rest = value - high
    middle = rest.astype(BF16).astype(F32)
    return high, middle, rest - middle


def stack_near(rows):
    high, middle, low = split_three(rows)
    return jnp.concatenate([high, high, high, middle, middle, low], axis=0).astype(BF16)


def stack_far(rows):
    high, middle, low = split_three(rows)
    return jnp.concatenate([high, middle, low, high, middle, high], axis=0).astype(BF16)


def bilinear(near_rows, far_rows):
    return lax.dot_general(
        stack_near(near_rows),
        stack_far(far_rows),
        (((0,), (0,)), ((), ())),
        preferred_element_type=F32,
    )


def moment_features(tile):
    row = lax.broadcasted_iota(jnp.int32, tile.shape, 0)
    by_x = tile * tile[0:1]
    by_y = jnp.where(row == 0, 1.0, tile * tile[1:2])
    by_z = tile * tile[2:3]
    whole = jnp.concatenate([tile, by_x, by_y, by_z], axis=0)
    high = whole.astype(BF16)
    low = (whole - high.astype(F32)).astype(BF16)
    both = jnp.concatenate([high, low], axis=0)
    return jnp.concatenate([both, both], axis=1)


def displacement(step_x, step_y, wrap):
    row = lax.broadcasted_iota(jnp.int32, (8, LEAF), 0)
    zero = jnp.zeros((8, LEAF), F32)
    out = jnp.where(row == 0, step_x, zero)
    out = jnp.where(row == 1, step_y, out)
    return jnp.where(row == 4, -wrap, out)


def finish_leaf(raw, tile):
    pos = [tile[k : k + 1] for k in range(3)]
    live = pos[0] < 0.5 * AWAY
    total = raw[16:17]
    first = [raw[k : k + 1] - pos[k] * total for k in range(3)]

    def second(left, right):
        lead = raw[8 + 8 * left + right : 9 + 8 * left + right]
        return lead - pos[left] * raw[right : right + 1] - pos[right] * first[left]

    density = jnp.where(live, total, 1.0)
    inverse_density = 1.0 / density

    def scaled(value):
        return jnp.where(live, value * inverse_density, 0.0)

    exx = scaled(second(0, 0)) + MOMENT_REG
    exy = scaled(second(0, 1))
    exz = scaled(second(0, 2))
    eyy = scaled(second(1, 1)) + MOMENT_REG
    eyz = scaled(second(1, 2))
    ezz = scaled(second(2, 2)) + MOMENT_REG
    mxx = eyy * ezz - eyz * eyz
    mxy = exz * eyz - exy * ezz
    mxz = exy * eyz - exz * eyy
    myy = exx * ezz - exz * exz
    myz = exy * exz - exx * eyz
    mzz = exx * eyy - exy * exy
    scale = 1.0 / (exx * mxx + exy * mxy + exz * mxz)
    inverse = [entry * scale for entry in (mxx, mxy, mxz, myy, myz, mzz)]
    square = inverse_density * inverse_density
    rows = [density] + [entry * square for entry in inverse]
    for quantity in range(3, 8):
        value = tile[quantity : quantity + 1]
        along = [
            scaled(
                raw[8 + 8 * k + quantity : 9 + 8 * k + quantity]
                - pos[k] * raw[quantity : quantity + 1]
                - value * first[k]
            )
            for k in range(3)
        ]
        half = [0.5 * term for term in along]
        rows.append(inverse[0] * half[0] + inverse[1] * half[1] + inverse[2] * half[2])
        rows.append(inverse[1] * half[0] + inverse[3] * half[1] + inverse[4] * half[2])
        rows.append(inverse[2] * half[0] + inverse[4] * half[1] + inverse[5] * half[2])
    rows.append(jnp.zeros((2, LEAF), F32))
    return jnp.concatenate(rows, axis=0)


def dot3(left, right):
    return left[0] * right[0] + left[1] * right[1] + left[2] * right[2]


def apply_sym(matrix, vector):
    return [
        dot3((matrix[0], matrix[1], matrix[2]), vector),
        dot3((matrix[1], matrix[3], matrix[4]), vector),
        dot3((matrix[2], matrix[4], matrix[5]), vector),
    ]


def stack_rows(rows):
    row = lax.broadcasted_iota(jnp.int32, (8, LEAF), 0)
    out = jnp.zeros((8, LEAF), F32)
    for k, entry in rows.items():
        out = jnp.where(row == k, entry, out)
    return out


def near_coefficients(tile, pay):
    pos = [tile[k : k + 1] for k in range(3)]
    twice = [(-2.0 / SUPPORT**2) * entry for entry in pos]
    out = [
        {
            0: dot3(pos, pos) * (1.0 / SUPPORT**2),
            1: twice[0],
            2: twice[1],
            3: twice[2],
            7: 1.0 / SUPPORT**2,
        }
    ]
    matrix = [pay[1 + k : 2 + k] for k in range(6)]
    for line in ((0, 1, 2), (1, 3, 4), (2, 4, 5)):
        entries = [matrix[k] for k in line]
        out.append({0: -dot3(entries, pos), 1: entries[0], 2: entries[1], 3: entries[2]})
    for quantity in range(5):
        slope = [pay[7 + 3 * quantity + k : 8 + 3 * quantity + k] for k in range(3)]
        value = tile[3 + quantity : 4 + quantity]
        if quantity < 3:
            entry = {0: 0.5 * value - dot3(slope, pos), 4 + quantity: -0.5}
        else:
            entry = {0: value - dot3(slope, pos)}
        entry.update({1: slope[0], 2: slope[1], 3: slope[2]})
        out.append(entry)
    return [stack_rows(entry) for entry in out]


def far_coefficients(tile, pay):
    pos = [tile[k : k + 1] for k in range(3)]
    out = []
    matrix = [pay[1 + k : 2 + k] for k in range(6)]
    for line in ((0, 1, 2), (1, 3, 4), (2, 4, 5)):
        entries = [matrix[k] for k in line]
        out.append({0: dot3(entries, pos), 1: -entries[0], 2: -entries[1], 3: -entries[2]})
    for quantity in range(5):
        slope = [pay[7 + 3 * quantity + k : 8 + 3 * quantity + k] for k in range(3)]
        value = tile[3 + quantity : 4 + quantity]
        if quantity < 3:
            entry = {0: 0.5 * value - dot3(slope, pos), 4 + quantity: -0.5}
        else:
            entry = {0: value - dot3(slope, pos)}
        entry.update({1: slope[0], 2: slope[1], 3: slope[2]})
        out.append(entry)
    return [stack_rows(entry) for entry in out]


def limited(value, low, high):
    return jnp.minimum(jnp.maximum(value, low), high)


def face_fluxes(near_out, far_out, toward, near_plain, far_plain):
    smooth = smoothing_of(near_out[0], KERNEL_NORM / AREA_FLOOR)
    length_sq = jnp.maximum(dot3(toward, toward), 1e-30)
    inverse_length = lax.rsqrt(length_sq)
    area = smooth * (length_sq * inverse_length)
    scale = jnp.minimum(inverse_length, smooth)
    normal = [entry * scale for entry in toward]
    left_vel, right_vel = [], []
    for k in range(3):
        high = jnp.abs(far_plain[k] - near_plain[k])
        low = -high
        left_vel.append(limited(near_out[1 + k], low, high))
        right_vel.append(limited(far_out[k], low, high))
    face_vel = [near_plain[k] + far_plain[k] for k in range(3)]
    thermo = []
    for k in range(2):
        low = jnp.minimum(near_plain[3 + k], far_plain[3 + k])
        high = jnp.maximum(near_plain[3 + k], far_plain[3 + k])
        thermo.append(limited(near_out[4 + k], low, high))
        thermo.append(limited(far_out[3 + k], low, high))
    left_rho, right_rho, left_p, right_p = thermo
    left_u = dot3(left_vel, normal)
    right_u = dot3(right_vel, normal)
    left_gp = GAMMA * left_p
    right_gp = GAMMA * right_p
    left_c = left_gp * lax.rsqrt(left_gp * left_rho)
    right_c = right_gp * lax.rsqrt(right_gp * right_rho)
    slow = jnp.minimum(left_u - left_c, right_u - right_c)
    fast = jnp.maximum(left_u + left_c, right_u + right_c)
    left_m = left_rho * (slow - left_u)
    right_m = right_rho * (fast - right_u)
    contact = (right_p - left_p + left_m * left_u - right_m * right_u) * reciprocal(
        left_m - right_m
    )
    is_left = contact >= 0.0
    speed = jnp.where(is_left, jnp.minimum(slow, 0.0), jnp.maximum(fast, 0.0))
    rho = jnp.where(is_left, left_rho, right_rho) * area
    press = jnp.where(is_left, left_p, right_p) * area
    normal_speed = jnp.where(is_left, left_u, right_u)
    vel = [jnp.where(is_left, left_vel[k], right_vel[k]) + face_vel[k] for k in range(3)]
    lag = speed - normal_speed
    ratio = lag * reciprocal(speed - contact)
    through = ratio * contact
    gain = speed * ratio - speed
    push = (rho * lag) * gain
    mass = rho * through
    total_p = press + push
    mom = [mass * vel[k] + total_p * normal[k] for k in range(3)]
    energy = press * (through * (1.0 / (GAMMA - 1.0)) + normal_speed + gain) + push * contact
    energy = energy + (0.5 * mass) * dot3(vel, vel) + total_p * dot3(face_vel, normal)
    return [mass] + mom + [energy]


def pack_kernel(
    width,
    leaf_sub,
    counts,
    positions,
    velocity,
    density,
    pressure,
    pair_list,
    state,
    listed,
):
    slab = lax.axis_index("slab")
    centre_x = slab.astype(F32) + 0.5
    row = lax.broadcasted_iota(jnp.int32, (3, LEAF), 0)
    lane = lax.broadcasted_iota(jnp.int32, (3, LEAF), 1)

    def one_leaf(column, carry):
        lanes = pl.ds(pl.multiple_of(column * LEAF, LEAF), LEAF)
        centre_y = column.astype(F32) + 0.5
        centre = jnp.where(row == 0, centre_x, jnp.where(row == 1, centre_y, 0.5))
        dead = (row == 0) & (lane >= counts[column])
        state[0:3, lanes] = jnp.where(dead, AWAY, positions[:, lanes] - centre)
        state[3:6, lanes] = velocity[:, lanes]
        state[6:7, lanes] = density[:, lanes]
        state[7:8, lanes] = pressure[:, lanes]
        return carry

    lax.fori_loop(0, width, one_leaf, 0, unroll=4)
    listed[...] = jnp.zeros(listed.shape, F32)
    slots = pair_list.shape[1]
    heads = pair_list[0:1, :]
    tails = pair_list[1:2, :]
    offsets = pair_list[2:3, :]
    occupied = heads >= 0
    head_col = heads - slab * width
    inside = (tails >= slab * width) & (tails < (slab + 1) * width)
    next_slab = lax.rem(slab + 1, lax.axis_size("slab"))
    tail_col = jnp.where(inside, tails - slab * width, tails - next_slab * width)
    outside = occupied & jnp.logical_not(inside)
    wraps = outside & (tails < heads)
    step_y = tail_col + offsets - head_col
    empty = 4 * width
    here = slice(0, slots)
    listed[0:1, here] = jnp.where(occupied, head_col, empty).astype(F32)
    listed[1:2, here] = jnp.where(
        occupied, jnp.where(inside, tail_col, tail_col + width), empty
    ).astype(F32)
    listed[2:3, here] = jnp.where(occupied, step_y, 0).astype(F32)
    listed[3:4, here] = jnp.where(wraps, 1.0, 0.0)
    seats = head_col - lax.axis_index("sub") * leaf_sub
    behind = lax.broadcasted_iota(jnp.int32, (1, leaf_sub + 1), 1)
    shifts = lax.rem(5 * width * LEAF - offsets, width)
    shift = jnp.max(jnp.where(outside, shifts, 0), axis=1, keepdims=True).astype(F32)
    facts = jnp.where(behind == leaf_sub, shift, 0.0)
    for k in range(leaf_sub):
        found = jnp.where(occupied & (seats == k), 1.0, 0.0)
        facts = jnp.where(behind == k, jnp.sum(found, axis=1, keepdims=True), facts)
    listed[3:4, slots : slots + leaf_sub + 1] = facts


def step_kernel(
    width,
    sub_count,
    slots,
    rec,
    counts,
    lower_ref,
    own_ref,
    upper_ref,
    beyond_ref,
    own_out,
    next_out,
    order,
    mine,
    need,
    costs,
    item_left,
    item_index,
    item_seat,
    local,
    raw,
    pay,
    far_coef,
    near_left,
    far_left,
    toward_left,
    near_plane,
    near_right,
    far_right,
    toward_right,
    far_half,
    spread,
    dist,
    near_form,
    far_form,
    toward_form,
    col_sum,
    row_sum,
    row_rate,
):
    whole = 4 * width
    leaf_sub = width // sub_count
    cap = 2 * leaf_sub
    stride = rec.shape[0] // (12 * sub_count)
    block = 4 * stride

    def slot_home(slot):
        return rec[slot]

    def slot_other(slot):
        return rec[slot + stride]

    def slot_step_y(slot):
        return rec[slot + 2 * stride].astype(F32)

    def slot_wrap(slot):
        return rec[slot + 3 * stride].astype(F32)

    def load_leaf(column, carry):
        lanes = pl.ds(pl.multiple_of(column * LEAF, LEAF), LEAF)
        local[column] = lower_ref[:, lanes]
        local[width + column] = own_ref[:, lanes]
        local[2 * width + column] = upper_ref[:, lanes]
        local[3 * width + column] = beyond_ref[:, lanes]
        for k in range(5):
            own_out[pl.ds(k * width + column, 1), :] = jnp.zeros((1, LEAF), F32)
            next_out[pl.ds(k * width + column, 1), :] = jnp.zeros((1, LEAF), F32)
        for slab in range(4):
            raw[slab * width + column] = jnp.zeros((32, LEAF), F32)
            need[slab * width + column] = 0
            need[(slab + 3) * width + column] = 0
        return carry

    lax.fori_loop(0, width, load_leaf, 0)
    local[whole] = jnp.zeros((8, LEAF), F32)
    raw[whole] = jnp.zeros((32, LEAF), F32)
    need[7 * width] = 0

    me = lax.axis_index("sub")
    total_cost = jnp.int32(0)
    shift_w = jnp.int32(0)
    for group in range(sub_count):
        seats = jnp.bitwise_xor(me, group) * leaf_sub
        facts = (3 * group + 1) * block + 3 * stride + slots
        shift_w = jnp.maximum(shift_w, rec[facts + leaf_sub])
        for k in range(leaf_sub):
            parts = lax.shift_right_logical(counts[seats + k] + (ROWS - 1), ROWS_LOG)
            cost = COST_LEAF + rec[facts + k] * (COST_SLOT + COST_PART * parts)
            costs[seats + k] = cost
            total_cost = total_cost + cost

    def deal(column, state):
        owner, length, before, first, mine_length = state
        cost = costs[column]
        middle = sub_count * (2 * before + cost)
        wish = (middle >= 2 * total_cost * (owner + 1)) | (length == cap)
        allowed = (owner < sub_count - 1) & (width - column <= (sub_count - 1 - owner) * cap)
        step = (wish & allowed).astype(jnp.int32)
        owner = owner + step
        length = (1 - step) * length + 1
        is_mine = (owner == me).astype(jnp.int32)
        first = jnp.where((is_mine > 0) & (mine_length == 0), column, first)
        return owner, length, before + cost, first, mine_length + is_mine

    zero = jnp.int32(0)
    _, _, _, base, length = lax.fori_loop(
        0, width, deal, (zero, zero, zero, zero, zero), unroll=4
    )
    upper_base = lax.rem(base + width - 1 + shift_w, width)

    def own_leaf(k):
        return width + lax.rem(base + k, width)

    def upper_leaf(k):
        return 2 * width + lax.rem(upper_base + k, width)

    def mark_own(k, carry):
        need[own_leaf(k)] = jnp.where(k < length, 3, 1)
        return carry

    def mark_upper(k, carry):
        need[upper_leaf(k)] = 1
        return carry

    lax.fori_loop(0, length + 1, mark_own, 0)
    lax.fori_loop(0, length + 2, mark_upper, 0)

    def collect_lower(k, carry):
        used, first = carry
        order[used] = first + k
        return used + (need[slot_other(first + k)] & 1), first

    def collect_own(k, carry):
        used, kept, first = carry
        slot = first + k
        flags = need[width + slot_home(slot)]
        order[used] = slot
        mine[kept] = slot
        used = used + ((flags | need[width + slot_other(slot)]) & 1)
        return used, kept + lax.shift_right_logical(flags, 1), first

    def collect_upper(k, carry):
        used, first = carry
        slot = first + k
        order[used] = slot
        flags = need[2 * width + slot_home(slot)] | need[2 * width + slot_other(slot)]
        return used + (flags & 1), first

    used, kept = zero, zero
    for group in range(sub_count):
        used, _ = lax.fori_loop(0, slots, collect_lower, (used, 3 * group * block), unroll=8)
    from_own = used
    for group in range(sub_count):
        used, kept, _ = lax.fori_loop(
            0, slots, collect_own, (used, kept, (3 * group + 1) * block), unroll=8
        )
    from_upper = used
    for group in range(sub_count):
        used, _ = lax.fori_loop(
            0, slots, collect_upper, (used, (3 * group + 2) * block), unroll=8
        )
    for extra in range(2 * UNROLL):
        order[used + extra] = -1

    def slab_base(position):
        return jnp.where(position < from_own, 0, jnp.where(position < from_upper, width, 2 * width))

    def clear_rows(seat, carry):
        for part in range(LEAF // ROWS):
            for k in range(5):
                row_sum[seat * (LEAF // ROWS) + part, k] = jnp.zeros((ROWS, LEAF), F32)
        return carry

    lax.fori_loop(0, length, clear_rows, 0)

    def clear_cols(seat, carry):
        col_sum[seat] = jnp.zeros((40, LEAF), F32)
        return carry

    lax.fori_loop(0, length + 1, clear_cols, 0)
    lax.fori_loop(cap + 1, cap + length + 3, clear_cols, 0)

    def slot_tiles(position):
        named = order[position]
        slot = jnp.maximum(named, 0)
        start = slab_base(position)
        other = slot_other(slot)
        shift = displacement(
            jnp.where(other >= width, 1.0, 0.0).astype(F32), slot_step_y(slot), slot_wrap(slot)
        )
        home = jnp.where(named < 0, whole, start + slot_home(slot))
        other = jnp.where(named < 0, whole, start + other)
        return home, other, local[home], local[other] + shift, shift

    def distances(group):
        row = lax.broadcasted_iota(jnp.int32, (8, LEAF), 0)
        for k in range(UNROLL):
            _, _, near, far, _ = slot_tiles(group * UNROLL + k)
            near_pos = [near[j : j + 1] for j in range(3)]
            far_pos = [far[j : j + 1] for j in range(3)]
            near_k = jnp.where(
                row < 3,
                near,
                jnp.where(row == 3, dot3(near_pos, near_pos), jnp.where(row == 4, 1.0, 0.0)),
            )
            far_k = jnp.where(
                row < 3,
                (-2.0 / SUPPORT**2) * far,
                jnp.where(
                    row == 4,
                    dot3(far_pos, far_pos) * (1.0 / SUPPORT**2),
                    jnp.where(row == 3, 1.0 / SUPPORT**2, 0.0),
                ),
            )
            dist[k] = bilinear(near_k, far_k)

    def moment_group(group, carry):
        parts = []
        for k in range(UNROLL):
            home, other, near, far, shift = slot_tiles(group * UNROLL + k)
            weight = jnp.where(home == other, 0.5, 1.0).astype(F32)
            smooth = smoothing_of(dist[k], KERNEL_NORM * weight)
            high = smooth.astype(BF16)
            low = (smooth - high.astype(F32)).astype(BF16)
            row_part = lax.dot_general(
                moment_features(far),
                jnp.concatenate([high, low], axis=1),
                (((1,), (1,)), ((), ())),
                preferred_element_type=F32,
            )
            col_part = lax.dot_general(
                moment_features(near - shift),
                jnp.concatenate([high, low], axis=0),
                (((1,), (0,)), ((), ())),
                preferred_element_type=F32,
            )
            parts.append((home, other, row_part, col_part))
        distances(group + 1)
        for home, other, row_part, col_part in parts:
            raw[home] += row_part[:32] + row_part[32:]
            raw[other] += col_part[:32] + col_part[32:]
        return carry

    distances(0)
    lax.fori_loop(0, (used + UNROLL - 1) // UNROLL, moment_group, 0)

    def window_leaf(seat):
        return jnp.where(seat <= cap, own_leaf(seat), upper_leaf(seat - cap - 1))

    def finish(seat, carry):
        leaf = window_leaf(seat)
        payload = finish_leaf(raw[leaf], local[leaf])
        pay[seat] = payload
        for k, entry in enumerate(far_coefficients(local[leaf], payload)):
            far_coef[seat, 8 * k : 8 * k + 8] = entry
        return carry

    lax.fori_loop(0, length + 1, finish, 0)
    lax.fori_loop(cap + 1, cap + length + 3, finish, 0)

    splits = LEAF // ROWS

    picked = lax.broadcasted_iota(jnp.int32, (48, LEAF), 0)
    for k in range(5):
        chosen = (picked == 3 + k) | (picked == 27 + k) | (picked == 43 + k)
        spread[:, k * LEAF : (k + 1) * LEAF] = jnp.where(chosen, 0.5 if k < 3 else 1.0, 0.0).astype(
            BF16
        )

    def turn_home(seat):
        tile = local[own_leaf(seat)]
        generic = {0: 1.0}
        generic.update({1 + k: tile[k : k + 1] for k in range(6)})
        generic = stack_near(stack_rows(generic))
        coefficients = [stack_near(entry) for entry in near_coefficients(tile, pay[seat])]
        planes = jnp.dot(stack_near(tile).T, spread[...], preferred_element_type=F32)
        turned_far = generic.T
        turned_near = [coefficients[k].T for k in (0, 4, 5, 6, 7, 8)]
        turned_toward = [
            jnp.concatenate([coefficients[1 + k], generic], axis=0).T for k in range(3)
        ]
        for part in range(splits):
            rows = slice(part * ROWS, (part + 1) * ROWS)
            place = seat * splits + part
            for k in range(6):
                near_left[place, k * ROWS : (k + 1) * ROWS, 0:48] = turned_near[k][rows]
            for k in range(3):
                toward_left[place, k * ROWS : (k + 1) * ROWS, 0:96] = turned_toward[k][rows]
            far_left[place, :, 0:48] = turned_far[rows]
            for k in range(5):
                near_plane[place, k] = planes[rows, k * LEAF : (k + 1) * LEAF]

    def turn_two(pair, carry):
        turn_home(2 * pair)
        turn_home(2 * pair + 1)
        return carry

    lax.fori_loop(0, (length + 1) // 2, turn_two, 0)

    def prepare_slot(index, count):
        slot = mine[index]
        valid = (index < kept).astype(jnp.int32)
        column = slot_home(slot)
        away = slot_other(slot)
        is_upper = away >= width
        other = width + away
        step_x = jnp.where(is_upper, 1.0, 0.0).astype(F32)
        step_y = slot_step_y(slot)
        wrap = slot_wrap(slot)
        other_seat = jnp.where(
            is_upper,
            cap + 1 + lax.rem(away - upper_base, width),
            lax.rem(away + width - base, width),
        )
        for part in range(splits):
            item_left[count] = (column - base) * splits + part
            item_index[count] = index
            item_seat[count] = jnp.where(column == away, -1 - other_seat, other_seat)
            count = count + valid * (counts[column] > part * ROWS).astype(jnp.int32)

        far = local[other] + displacement(step_x, step_y, wrap)
        row = lax.broadcasted_iota(jnp.int32, (8, LEAF), 0)
        pos = [far[k : k + 1] for k in range(3)]
        generic = {0: 1.0, 7: dot3(pos, pos)}
        generic.update({1 + k: far[k : k + 1] for k in range(6)})
        generic = stack_far(stack_rows(generic))
        near_right[index] = generic
        for k in range(8):
            entry = far_coef[other_seat, 8 * k : 8 * k + 8]
            change = entry[1:2] * step_x + entry[2:3] * step_y
            if k == 4:
                change = change + 0.5 * wrap
            entry = stack_far(jnp.where(row == 0, entry - change, entry))
            if k < 3:
                toward_right[index, 0:48, k * LEAF : (k + 1) * LEAF] = generic
                toward_right[index, 48:96, k * LEAF : (k + 1) * LEAF] = entry
            else:
                far_right[index, :, (k - 3) * LEAF : (k - 2) * LEAF] = entry
        far_half[index, 0:5] = jnp.concatenate([0.5 * far[3:6], far[6:8]], axis=0)
        return count

    def prepare_two(pair, count):
        return prepare_slot(2 * pair + 1, prepare_slot(2 * pair, count))

    mine[kept] = mine[0]
    item_count = lax.fori_loop(0, (kept + 1) // 2, prepare_two, 0)
    item_left[item_count] = 0
    item_index[item_count] = 0

    def forms(position):
        index = item_index[position]
        left = item_left[position]
        near_form[...] = jnp.dot(
            near_left[left, :, 0:48], near_right[index], preferred_element_type=F32
        )
        far_form[...] = jnp.dot(
            far_left[left, :, 0:48], far_right[index], preferred_element_type=F32
        )
        for k in range(3):
            toward_form[k * ROWS : (k + 1) * ROWS, :] = jnp.dot(
                toward_left[left, k * ROWS : (k + 1) * ROWS, 0:96],
                toward_right[index, :, k * LEAF : (k + 1) * LEAF],
                preferred_element_type=F32,
            )

    def flux_item(position, carry):
        left = item_left[position]
        index = item_index[position]
        coded = item_seat[position]
        other_seat = jnp.where(coded < 0, -1 - coded, coded)
        weight = jnp.where(coded < 0, 0.0, 1.0).astype(F32)
        fluxes = face_fluxes(
            [near_form[k * ROWS : (k + 1) * ROWS, :] for k in range(6)],
            [far_form[:, k * LEAF : (k + 1) * LEAF] for k in range(5)],
            [toward_form[k * ROWS : (k + 1) * ROWS, :] for k in range(3)],
            [near_plane[left, k] for k in range(5)],
            [far_half[index, k : k + 1, :] for k in range(5)],
        )
        forms(position + 1)
        for k in range(5):
            row_sum[left, k] += fluxes[k]
            col_sum[other_seat, 8 * k : 8 * k + 8] += weight * sum(
                fluxes[k][8 * j : 8 * j + 8] for j in range(ROWS // 8)
            )
        return carry

    forms(0)
    lax.fori_loop(0, item_count, flux_item, 0)

    lane = lax.broadcasted_iota(jnp.int32, (ROWS, LEAF), 1)

    def row_total(seat, carry):
        pieces = []
        for part in range(splits):
            total = jnp.zeros((ROWS, LEAF), F32)
            for c in range(5):
                reduced = jnp.sum(row_sum[seat * splits + part, c], axis=1, keepdims=True)
                total = jnp.where(lane == c, reduced, total)
            pieces.append(total)
        row_rate[seat] = jnp.concatenate(pieces, axis=0).T[0:8]
        return carry

    lax.fori_loop(0, length, row_total, 0)
    row_rate[length] = jnp.zeros((8, LEAF), F32)

    def rates(seat, less):
        leaf = window_leaf(seat)
        total = stack_rows(
            {
                k: jnp.sum(col_sum[seat, 8 * k : 8 * k + 8], axis=0, keepdims=True)
                for k in range(5)
            }
        )
        if less is not None:
            total = total - less
        live = local[leaf][0:1] < 0.5 * AWAY
        scale = AREA_FLOOR * pay[seat][0:1]
        return lax.rem(leaf, width), jnp.where(live, total * scale, 0.0)

    def write_own(k, carry):
        column, value = rates(k, row_rate[k])
        for c in range(5):
            own_out[pl.ds(c * width + column, 1), :] = value[c : c + 1]
        return carry

    def write_upper(k, carry):
        column, value = rates(k, None)
        for c in range(5):
            next_out[pl.ds(c * width + column, 1), :] = value[c : c + 1]
        return carry

    lax.fori_loop(0, length + 1, write_own, 0)
    lax.fori_loop(cap + 1, cap + length + 3, write_upper, 0)


def shards(positions, velocity, density, pressure, counts, pair_list):
    width = counts.shape[0]
    slots = pair_list.shape[1]
    particles = width * LEAF
    sub_count = lax.axis_size("sub")
    leaf_sub = width // sub_count

    smem = pl.BlockSpec(memory_space=pltpu.SMEM)
    vmem = pl.BlockSpec(memory_space=pltpu.VMEM)
    lanes = -(-(slots + leaf_sub + 1) // LEAF) * LEAF
    state, listed = pl.pallas_call(
        functools.partial(pack_kernel, width, leaf_sub),
        out_shape=[
            jax.ShapeDtypeStruct((8, particles), F32),
            jax.ShapeDtypeStruct((4, lanes), F32),
        ],
        in_specs=[smem, vmem, vmem, vmem, vmem, vmem],
        out_specs=[vmem, vmem],
        name="pack",
    )(
        counts,
        positions,
        velocity,
        density[None],
        pressure[None],
        pair_list,
    )
    lists = jnp.stack([shifted(listed, "slab", 1), listed, shifted(listed, "slab", -1)])[None]
    lower = shifted(state, "slab", 1)
    upper = shifted(state, "slab", -1)
    beyond = shifted(state, "slab", -2)
    mask = 1
    while mask < sub_count:
        lists = jnp.concatenate([lists, swapped(lists, "sub", mask)], axis=0)
        mask *= 2
    rec = lists.astype(jnp.int32).reshape(-1)
    cap = 2 * leaf_sub
    most = cap * CAND
    splits = LEAF // ROWS

    own_part, next_part = pl.pallas_call(
        functools.partial(step_kernel, width, sub_count, slots),
        out_shape=[jax.ShapeDtypeStruct((5 * width, LEAF), F32)] * 2,
        in_specs=[smem, smem, vmem, vmem, vmem, vmem],
        out_specs=[vmem, vmem],
        scratch_shapes=[
            pltpu.SMEM((3 * sub_count * slots + 2 * UNROLL,), jnp.int32),
            pltpu.SMEM((most + 1,), jnp.int32),
            pltpu.SMEM((7 * width + 1,), jnp.int32),
            pltpu.SMEM((width,), jnp.int32),
        ]
        + [pltpu.SMEM((most * splits + 1,), jnp.int32)] * 3
        + [
            pltpu.VMEM((4 * width + 1, 8, LEAF), F32),
            pltpu.VMEM((4 * width + 1, 32, LEAF), F32),
            pltpu.VMEM((2 * cap + 3, 24, LEAF), F32),
            pltpu.VMEM((2 * cap + 3, 64, LEAF), F32),
            pltpu.VMEM((cap * splits, 6 * ROWS, LEAF), BF16),
            pltpu.VMEM((cap * splits, ROWS, LEAF), BF16),
            pltpu.VMEM((cap * splits, 3 * ROWS, LEAF), BF16),
            pltpu.VMEM((cap * splits, 5, ROWS, LEAF), F32),
            pltpu.VMEM((most, 48, LEAF), BF16),
            pltpu.VMEM((most, 48, 5 * LEAF), BF16),
            pltpu.VMEM((most, 96, 3 * LEAF), BF16),
            pltpu.VMEM((most, 8, LEAF), F32),
            pltpu.VMEM((48, 5 * LEAF), BF16),
            pltpu.VMEM((UNROLL, LEAF, LEAF), F32),
            pltpu.VMEM((6 * ROWS, LEAF), F32),
            pltpu.VMEM((ROWS, 5 * LEAF), F32),
            pltpu.VMEM((3 * ROWS, LEAF), F32),
            pltpu.VMEM((2 * cap + 3, 40, LEAF), F32),
            pltpu.VMEM((cap * splits, 5, ROWS, LEAF), F32),
            pltpu.VMEM((cap + 1, 8, LEAF), F32),
        ],
        compiler_params=pltpu.CompilerParams(vmem_limit_bytes=48 * 1024 * 1024),
        name="hydro_step",
    )(rec, counts, lower, state, upper, beyond)

    merged = own_part + shifted(next_part, "slab", 1)
    mask = 1
    while mask < sub_count:
        merged = merged + swapped(merged, "sub", mask)
        mask *= 2
    return merged.reshape(5, particles)


def solution(mesh):
    placed = (
        P(None, "slab"),
        P(None, "slab"),
        P("slab"),
        P("slab"),
        P("slab"),
        P(None, ("slab", "sub")),
    )
    return jax.shard_map(
        shards, mesh=mesh, in_specs=placed, out_specs=P(None, "slab"), check_vma=False
    )
```

profile of v0, /device:TPU:0, one launch (start us, length us, event | category | flops | bytes accessed | tf_op | source)
XLA Modules:
  0.0 72.0 jit_solution(13625300860081198461)
XLA Ops:
  0.0 1.9 %pack.1 = (f32[8,4096]{1,0:T(8,128)}, f32[4,128]{1,0:T(4,128)}) custom-call(s32[32]{0:T(128)} %counts.3, f32[3,4096]{1,0:T(4,128)} %positions.1, f32[3,4096]{1,0:T(4,128)} %velocity.1, f32[1,4096]{1,0:T(1,128)} %bitcast.9, f32[1,4096]{1,0:T(1,128)} %bitcast.10, s32[3,40]{1,0:T(4,128)} %pair_list.1), custom_call_target="tpu_custom_call" | custom-call | tf_op jit(solution)/shard_map/pack/pallas_call | solution.py:776
  1.9 3.3 %collective-permute-start.1 = (f32[4,128]{1,0:T(4,128)}, f32[4,128]{1,0:T(4,128)S(1)}, u32[]{:S(2)}, u32[]{:S(2)}) collective-permute-start(f32[4,128]{1,0:T(4,128)} %get-tuple-element.9), channel_id=1, source_target_pairs={{0,28},{4,0},{8,4},{12,8},{16,12},{20,16},{24,20},{28,24},{1,29},{... | collective-permute-start | bytes 6152 | tf_op jit(solution)/shard_map/ppermute | solution.py:30
  5.2 0.0 collective-permute-start
  5.2 1.5 %collective-permute-done.1 = f32[4,128]{1,0:T(4,128)S(1)} collective-permute-done((f32[4,128]{1,0:T(4,128)}, f32[4,128]{1,0:T(4,128)S(1)}, u32[]{:S(2)}, u32[]{:S(2)}) %collective-permute-start.1) | collective-permute-done | bytes 2080 | tf_op jit(solution)/shard_map/ppermute | solution.py:30
  6.7 2.6 %collective-permute-done = f32[4,128]{1,0:T(4,128)S(1)} collective-permute-done((f32[4,128]{1,0:T(4,128)}, f32[4,128]{1,0:T(4,128)S(1)}, u32[]{:S(2)}, u32[]{:S(2)}) %collective-permute-start) | collective-permute-done | bytes 2080 | tf_op jit(solution)/shard_map/ppermute | solution.py:30
  9.3 0.0 copy-start.2
  9.3 0.7 copy-done.2
  10.0 1.6 %collective-permute-start.2 = (f32[1,3,4,128]{3,2,1,0:T(4,128)S(1)}, f32[1,3,4,128]{3,2,1,0:T(4,128)S(1)}, u32[]{:S(2)}, u32[]{:S(2)}) collective-permute-start(f32[1,3,4,128]{3,2,1,0:T(4,128)S(1)} %maximum_bitcast_fusion), channel_id=1, source_target_pairs={{0,1},{1,0},{2,3},{3,2},{4,5},{5,4},{6,7},{7,6},{8,9},{9,8},{10,11... | collective-permute-start | bytes 18440 | tf_op jit(solution)/shard_map/ppermute | solution.py:35
  11.6 0.0 collective-permute-start.6
  11.6 0.0 collective-permute-start.5
  11.6 0.5 collective-permute-start.4
  12.1 1.5 %collective-permute-done.2 = f32[1,3,4,128]{3,2,1,0:T(4,128)S(1)} collective-permute-done((f32[1,3,4,128]{3,2,1,0:T(4,128)S(1)}, f32[1,3,4,128]{3,2,1,0:T(4,128)S(1)}, u32[]{:S(2)}, u32[]{:S(2)}) %collective-permute-start.2) | collective-permute-done | bytes 6176 | tf_op jit(solution)/shard_map/ppermute | solution.py:35
  13.6 2.6 %collective-permute-start.3 = (f32[2,3,4,128]{3,2,1,0:T(4,128)S(1)}, f32[2,3,4,128]{3,2,1,0:T(4,128)S(1)}, u32[]{:S(2)}, u32[]{:S(2)}) collective-permute-start(f32[2,3,4,128]{3,2,1,0:T(4,128)S(1)} %pad_maximum_fusion), channel_id=1, source_target_pairs={{0,2},{1,3},{2,0},{3,1},{4,6},{5,7},{6,4},{7,5},{8,10},{9,11},{10,... | collective-permute-start | bytes 36872 | tf_op jit(solution)/shard_map/ppermute | solution.py:35
  16.2 2.0 %collective-permute-done.3 = f32[2,3,4,128]{3,2,1,0:T(4,128)S(1)} collective-permute-done((f32[2,3,4,128]{3,2,1,0:T(4,128)S(1)}, f32[2,3,4,128]{3,2,1,0:T(4,128)S(1)}, u32[]{:S(2)}, u32[]{:S(2)}) %collective-permute-start.3) | collective-permute-done | bytes 12320 | tf_op jit(solution)/shard_map/ppermute | solution.py:35
  18.3 0.0 copy-start.1
  18.3 0.0 collective-permute-done.6.beyond_ref
  18.3 0.0 collective-permute-done.5.upper_ref
  18.3 0.1 collective-permute-done.4.lower_ref
  18.4 0.5 copy-done.1
  18.9 0.0 copy-start
  18.9 0.9 %copy-done = f32[8,4096]{1,0:T(8,128)S(1)} copy-done((f32[8,4096]{1,0:T(8,128)S(1)}, f32[8,4096]{1,0:T(8,128)}, u32[]{:S(2)}) %copy-start) | copy-done | bytes 131096
  19.8 32.0 %hydro_step.1 = (f32[160,128]{1,0:T(8,128)S(1)}, f32[160,128]{1,0:T(8,128)S(1)}) custom-call(s32[6144]{0:T(1024)S(1)} %bitcast.8, s32[32]{0:T(128)S(1)} %copy-done.1, f32[8,4096]{1,0:T(8,128)S(1)} %collective-permute-done.4.lower_ref, f32[8,4096]{1,0:T(8,128)S(1)} %copy-done, f32[8,4096]{1,0:T(8,128)S(1)} %collective-permute-done.5.upper_ref, ...), custom_call_target="tpu_custom_call" | custom-call | tf_op jit(solution)/shard_map/hydro_step/pallas_call | solution.py:806
  51.8 3.6 %collective-permute-start.7 = (f32[160,128]{1,0:T(8,128)S(1)}, f32[160,128]{1,0:T(8,128)S(1)}, u32[]{:S(2)}, u32[]{:S(2)}) collective-permute-start(f32[160,128]{1,0:T(8,128)S(1)} %get-tuple-element.12), channel_id=1, source_target_pairs={{0,4},{4,8},{8,12},{12,16},{16,20},{20,24},{24,28},{28,0},{1,5},{5... | collective-permute-start | bytes 245768 | tf_op jit(solution)/shard_map/ppermute | solution.py:30
  55.4 1.2 %collective-permute-done.7 = f32[160,128]{1,0:T(8,128)S(1)} collective-permute-done((f32[160,128]{1,0:T(8,128)S(1)}, f32[160,128]{1,0:T(8,128)S(1)}, u32[]{:S(2)}, u32[]{:S(2)}) %collective-permute-start.7) | collective-permute-done | bytes 81952 | tf_op jit(solution)/shard_map/ppermute | solution.py:30
  56.6 0.1 collective-permute-start.8
  56.7 4.6 %collective-permute-done.8 = f32[160,128]{1,0:T(8,128)S(1)} collective-permute-done((f32[160,128]{1,0:T(8,128)S(1)}, f32[160,128]{1,0:T(8,128)S(1)}, u32[]{:S(2)}, u32[]{:S(2)}) %collective-permute-start.8) | collective-permute-done | bytes 81952 | tf_op jit(solution)/shard_map/ppermute | solution.py:35
  61.3 6.3 %collective-permute-start.9 = (f32[160,128]{1,0:T(8,128)S(1)}, f32[160,128]{1,0:T(8,128)S(1)}, u32[]{:S(2)}, u32[]{:S(2)}) collective-permute-start(f32[160,128]{1,0:T(8,128)S(1)} %add.10), channel_id=1, source_target_pairs={{0,2},{1,3},{2,0},{3,1},{4,6},{5,7},{6,4},{7,5},{8,10},{9,11},{10,... | collective-permute-start | bytes 245768 | tf_op jit(solution)/shard_map/ppermute | solution.py:35
  67.6 3.7 %collective-permute-done.9 = f32[160,128]{1,0:T(8,128)S(1)} collective-permute-done((f32[160,128]{1,0:T(8,128)S(1)}, f32[160,128]{1,0:T(8,128)S(1)}, u32[]{:S(2)}, u32[]{:S(2)}) %collective-permute-start.9) | collective-permute-done | bytes 81952 | tf_op jit(solution)/shard_map/ppermute | solution.py:35
  71.3 0.7 reshape.6
  (6 shorter events, 0.1 us)
Async XLA Ops:
  1.9 4.9 %collective-permute-start.1 = (f32[4,128]{1,0:T(4,128)}, f32[4,128]{1,0:T(4,128)S(1)}, u32[]{:S(2)}, u32[]{:S(2)}) collective-permute-start(f32[4,128]{1,0:T(4,128)} %get-tuple-element.9), channel_id=1, source_target_pairs={{0,28},{4,0},{8,4},{12,8},{16,12},{20,16},{24,20},{28,24},{1,29},{... | collective-permute-start | bytes 6152 | tf_op jit(solution)/shard_map/ppermute | solution.py:30
  5.2 4.1 %collective-permute-start = (f32[4,128]{1,0:T(4,128)}, f32[4,128]{1,0:T(4,128)S(1)}, u32[]{:S(2)}, u32[]{:S(2)}) collective-permute-start(f32[4,128]{1,0:T(4,128)} %get-tuple-element.9), channel_id=1, source_target_pairs={{0,4},{4,8},{8,12},{12,16},{16,20},{20,24},{24,28},{28,0},{1,5},{5... | collective-permute-start | bytes 6152 | tf_op jit(solution)/shard_map/ppermute | solution.py:30
  9.3 0.7 copy-start.2
  10.0 3.6 %collective-permute-start.2 = (f32[1,3,4,128]{3,2,1,0:T(4,128)S(1)}, f32[1,3,4,128]{3,2,1,0:T(4,128)S(1)}, u32[]{:S(2)}, u32[]{:S(2)}) collective-permute-start(f32[1,3,4,128]{3,2,1,0:T(4,128)S(1)} %maximum_bitcast_fusion), channel_id=1, source_target_pairs={{0,1},{1,0},{2,3},{3,2},{4,5},{5,4},{6,7},{7,6},{8,9},{9,8},{10,11... | collective-permute-start | bytes 18440 | tf_op jit(solution)/shard_map/ppermute | solution.py:35
  11.6 6.7 %collective-permute-start.6 = (f32[8,4096]{1,0:T(8,128)}, f32[8,4096]{1,0:T(8,128)S(1)}, u32[]{:S(2)}, u32[]{:S(2)}) collective-permute-start(f32[8,4096]{1,0:T(8,128)} %get-tuple-element.10.own_ref), channel_id=1, source_target_pairs={{0,24},{4,28},{8,0},{12,4},{16,8},{20,12},{24,16},{28,20},{1,25},{... | collective-permute-start | bytes 393224 | tf_op jit(solution)/shard_map/ppermute | solution.py:30
  11.6 6.7 %collective-permute-start.5 = (f32[8,4096]{1,0:T(8,128)}, f32[8,4096]{1,0:T(8,128)S(1)}, u32[]{:S(2)}, u32[]{:S(2)}) collective-permute-start(f32[8,4096]{1,0:T(8,128)} %get-tuple-element.10.own_ref), channel_id=1, source_target_pairs={{0,28},{4,0},{8,4},{12,8},{16,12},{20,16},{24,20},{28,24},{1,29},{... | collective-permute-start | bytes 393224 | tf_op jit(solution)/shard_map/ppermute | solution.py:30
  11.6 6.8 %collective-permute-start.4 = (f32[8,4096]{1,0:T(8,128)}, f32[8,4096]{1,0:T(8,128)S(1)}, u32[]{:S(2)}, u32[]{:S(2)}) collective-permute-start(f32[8,4096]{1,0:T(8,128)} %get-tuple-element.10.own_ref), channel_id=1, source_target_pairs={{0,4},{4,8},{8,12},{12,16},{16,20},{20,24},{24,28},{28,0},{1,5},{5... | collective-permute-start | bytes 393224 | tf_op jit(solution)/shard_map/ppermute | solution.py:30
  13.6 4.6 %collective-permute-start.3 = (f32[2,3,4,128]{3,2,1,0:T(4,128)S(1)}, f32[2,3,4,128]{3,2,1,0:T(4,128)S(1)}, u32[]{:S(2)}, u32[]{:S(2)}) collective-permute-start(f32[2,3,4,128]{3,2,1,0:T(4,128)S(1)} %pad_maximum_fusion), channel_id=1, source_target_pairs={{0,2},{1,3},{2,0},{3,1},{4,6},{5,7},{6,4},{7,5},{8,10},{9,11},{10,... | collective-permute-start | bytes 36872 | tf_op jit(solution)/shard_map/ppermute | solution.py:35
  18.3 0.7 copy-start.1
  18.9 0.9 %copy-start = (f32[8,4096]{1,0:T(8,128)S(1)}, f32[8,4096]{1,0:T(8,128)}, u32[]{:S(2)}) copy-start(f32[8,4096]{1,0:T(8,128)} %get-tuple-element.10.own_ref) | copy-start | bytes 393220
  51.8 4.8 %collective-permute-start.7 = (f32[160,128]{1,0:T(8,128)S(1)}, f32[160,128]{1,0:T(8,128)S(1)}, u32[]{:S(2)}, u32[]{:S(2)}) collective-permute-start(f32[160,128]{1,0:T(8,128)S(1)} %get-tuple-element.12), channel_id=1, source_target_pairs={{0,4},{4,8},{8,12},{12,16},{16,20},{20,24},{24,28},{28,0},{1,5},{5... | collective-permute-start | bytes 245768 | tf_op jit(solution)/shard_map/ppermute | solution.py:30
  56.6 4.7 %collective-permute-start.8 = (f32[160,128]{1,0:T(8,128)S(1)}, f32[160,128]{1,0:T(8,128)S(1)}, u32[]{:S(2)}, u32[]{:S(2)}) collective-permute-start(f32[160,128]{1,0:T(8,128)S(1)} %add.9), channel_id=1, source_target_pairs={{0,1},{1,0},{2,3},{3,2},{4,5},{5,4},{6,7},{7,6},{8,9},{9,8},{10,11... | collective-permute-start | bytes 245768 | tf_op jit(solution)/shard_map/ppermute | solution.py:35
  61.3 10.0 %collective-permute-start.9 = (f32[160,128]{1,0:T(8,128)S(1)}, f32[160,128]{1,0:T(8,128)S(1)}, u32[]{:S(2)}, u32[]{:S(2)}) collective-permute-start(f32[160,128]{1,0:T(8,128)S(1)} %add.10), channel_id=1, source_target_pairs={{0,2},{1,3},{2,0},{3,1},{4,6},{5,7},{6,4},{7,5},{8,10},{9,11},{10,... | collective-permute-start | bytes 245768 | tf_op jit(solution)/shard_map/ppermute | solution.py:35
where the time goes:
time: 71.2 us; the launch traced here: 72 us
  Pallas kernels  33.9 us (48%)
  starting transfers between devices  17.9 us (25%)
  waiting for transfers between devices  17.3 us (24%)
  local copies, waits for them, and re-layouts  2.75 us (4%)
    pallas_call x1, Pallas kernels, shards(): pl.pallas_call(functools.partial(step_kernel, width, sub_count, slots), o...  32 us
    ppermute x4, waiting for transfers between devices, swapped(): return lax.ppermute(shard, axis, [(i, i ^ mask) for i in range(peers)])  11.9 us
    ppermute x4, starting transfers between devices, swapped(): return lax.ppermute(shard, axis, [(i, i ^ mask) for i in range(peers)])  10.5 us
    ppermute x6, starting transfers between devices, shifted(): lax.ppermute(shard, axis, [(i, (i + by) % peers) for i in range(peers)])  7.44 us
    ppermute x6, waiting for transfers between devices, shifted(): lax.ppermute(shard, axis, [(i, (i + by) % peers) for i in range(peers)])  5.47 us
    unnamed x6, local copies, waits for them, and re-layouts  2.08 us
    pallas_call x1, Pallas kernels, shards(): pl.pallas_call(functools.partial(pack_kernel, width, leaf_sub), out_shape...  1.88 us
  transfers between devices with their start and end apart: 10, of which 8 were waited for; matrix products, arithmetic and copies ran while one was open for 0% of the time, Pallas kernels for 0%

commit v1 on v0

--- a/solution.py
+++ b/solution.py
@@ -214,25 +214,28 @@
     return jnp.minimum(jnp.maximum(value, low), high)
 
 
-def face_fluxes(near_out, far_out, toward, near_plain, far_plain):
-    smooth = smoothing_of(near_out[0], KERNEL_NORM / AREA_FLOOR)
+def face_geometry(dist_sq, toward):
+    smooth = smoothing_of(dist_sq, KERNEL_NORM / AREA_FLOOR)
     length_sq = jnp.maximum(dot3(toward, toward), 1e-30)
     inverse_length = lax.rsqrt(length_sq)
     area = smooth * (length_sq * inverse_length)
     scale = jnp.minimum(inverse_length, smooth)
-    normal = [entry * scale for entry in toward]
+    return [entry * scale for entry in toward] + [area]
+
+
+def face_fluxes(near_out, far_out, normal, area, near_plain, far_plain):
     left_vel, right_vel = [], []
     for k in range(3):
         high = jnp.abs(far_plain[k] - near_plain[k])
         low = -high
-        left_vel.append(limited(near_out[1 + k], low, high))
+        left_vel.append(limited(near_out[k], low, high))
         right_vel.append(limited(far_out[k], low, high))
     face_vel = [near_plain[k] + far_plain[k] for k in range(3)]
     thermo = []
     for k in range(2):
         low = jnp.minimum(near_plain[3 + k], far_plain[3 + k])
         high = jnp.maximum(near_plain[3 + k], far_plain[3 + k])
-        thermo.append(limited(near_out[4 + k], low, high))
+        thermo.append(limited(near_out[3 + k], low, high))
         thermo.append(limited(far_out[3 + k], low, high))
     left_rho, right_rho, left_p, right_p = thermo
     left_u = dot3(left_vel, normal)
@@ -271,6 +274,7 @@
     width,
     leaf_sub,
     counts,
+    counts_row,
     positions,
     velocity,
     density,
@@ -312,6 +316,7 @@
     empty = 4 * width
     here = slice(0, slots)
     listed[0:1, here] = jnp.where(occupied, head_col, empty).astype(F32)
+    listed[0:1, slots : slots + width] = counts_row[...].astype(F32)
     listed[1:2, here] = jnp.where(
         occupied, jnp.where(inside, tail_col, tail_col + width), empty
     ).astype(F32)
@@ -333,7 +338,6 @@
     sub_count,
     slots,
     rec,
-    counts,
     lower_ref,
     own_ref,
     upper_ref,
@@ -364,6 +368,8 @@
     near_form,
     far_form,
     toward_form,
+    dist_form,
+    geo_form,
     col_sum,
     row_sum,
     row_rate,
@@ -374,6 +380,9 @@
     stride = rec.shape[0] // (12 * sub_count)
     block = 4 * stride
 
+    def count_of(column):
+        return rec[block + slots + column]
+
     def slot_home(slot):
         return rec[slot]
 
@@ -386,24 +395,11 @@
     def slot_wrap(slot):
         return rec[slot + 3 * stride].astype(F32)
 
-    def load_leaf(column, carry):
-        lanes = pl.ds(pl.multiple_of(column * LEAF, LEAF), LEAF)
-        local[column] = lower_ref[:, lanes]
-        local[width + column] = own_ref[:, lanes]
-        local[2 * width + column] = upper_ref[:, lanes]
-        local[3 * width + column] = beyond_ref[:, lanes]
-        for k in range(5):
-            own_out[pl.ds(k * width + column, 1), :] = jnp.zeros((1, LEAF), F32)
-            next_out[pl.ds(k * width + column, 1), :] = jnp.zeros((1, LEAF), F32)
-        for slab in range(4):
-            raw[slab * width + column] = jnp.zeros((32, LEAF), F32)
-            need[slab * width + column] = 0
-            need[(slab + 3) * width + column] = 0
-        return carry
-
-    lax.fori_loop(0, width, load_leaf, 0)
-    local[whole] = jnp.zeros((8, LEAF), F32)
-    raw[whole] = jnp.zeros((32, LEAF), F32)
+    def clear_need(entry, carry):
+        need[entry] = 0
+        return carry
+
+    lax.fori_loop(0, 7 * width, clear_need, 0, unroll=16)
     need[7 * width] = 0
 
     me = lax.axis_index("sub")
@@ -414,7 +410,7 @@
         facts = (3 * group + 1) * block + 3 * stride + slots
         shift_w = jnp.maximum(shift_w, rec[facts + leaf_sub])
         for k in range(leaf_sub):
-            parts = lax.shift_right_logical(counts[seats + k] + (ROWS - 1), ROWS_LOG)
+            parts = lax.shift_right_logical(count_of(seats + k) + (ROWS - 1), ROWS_LOG)
             cost = COST_LEAF + rec[facts + k] * (COST_SLOT + COST_PART * parts)
             costs[seats + k] = cost
             total_cost = total_cost + cost
@@ -476,21 +472,68 @@
         flags = need[2 * width + slot_home(slot)] | need[2 * width + slot_other(slot)]
         return used + (flags & 1), first
 
+    def touches(first, last, start, count):
+        ahead = lax.rem(first - start + 4 * width, width) < count
+        return ahead | (lax.rem(start - first + 4 * width, width) <= last - first)
+
     used, kept = zero, zero
     for group in range(sub_count):
-        used, _ = lax.fori_loop(0, slots, collect_lower, (used, 3 * group * block), unroll=8)
+        first = jnp.bitwise_xor(me, group) * leaf_sub
+        slot = 3 * group * block
+        moved = first + rec[slot + 3 * stride + slots + leaf_sub]
+        used = lax.cond(
+            touches(moved - 1, moved + leaf_sub, base, length + 1),
+            lambda used, slot=slot: lax.fori_loop(
+                0, slots, collect_lower, (used, slot), unroll=8
+            )[0],
+            lambda used: used,
+            used,
+        )
     from_own = used
     for group in range(sub_count):
-        used, kept, _ = lax.fori_loop(
-            0, slots, collect_own, (used, kept, (3 * group + 1) * block), unroll=8
+        first = jnp.bitwise_xor(me, group) * leaf_sub
+        slot = (3 * group + 1) * block
+        used, kept = lax.cond(
+            touches(first - 1, first + leaf_sub, base - 1, length + 2),
+            lambda used, kept, slot=slot: lax.fori_loop(
+                0, slots, collect_own, (used, kept, slot), unroll=8
+            )[0:2],
+            lambda used, kept: (used, kept),
+            used,
+            kept,
         )
     from_upper = used
     for group in range(sub_count):
-        used, _ = lax.fori_loop(
-            0, slots, collect_upper, (used, (3 * group + 2) * block), unroll=8
+        first = jnp.bitwise_xor(me, group) * leaf_sub
+        slot = (3 * group + 2) * block
+        used = lax.cond(
+            touches(first, first + leaf_sub, upper_base, length + 2),
+            lambda used, slot=slot: lax.fori_loop(
+                0, slots, collect_upper, (used, slot), unroll=8
+            )[0],
+            lambda used: used,
+            used,
         )
     for extra in range(2 * UNROLL):
         order[used + extra] = -1
+
+    def load_leaf(column, carry):
+        lanes = pl.ds(pl.multiple_of(column * LEAF, LEAF), LEAF)
+        local[column] = lower_ref[:, lanes]
+        local[width + column] = own_ref[:, lanes]
+        local[2 * width + column] = upper_ref[:, lanes]
+        local[3 * width + column] = beyond_ref[:, lanes]
+        for k in range(5):
+            own_out[pl.ds(k * width + column, 1), :] = jnp.zeros((1, LEAF), F32)
+            next_out[pl.ds(k * width + column, 1), :] = jnp.zeros((1, LEAF), F32)
+        for slab in range(4):
+            raw[slab * width + column] = jnp.zeros((32, LEAF), F32)
+        return carry
+
+    lax.fori_loop(0, width, load_leaf, 0)
+    local[whole] = jnp.zeros((8, LEAF), F32)
+    raw[whole] = jnp.zeros((32, LEAF), F32)
+
 
     def slab_base(position):
         return jnp.where(position < from_own, 0, jnp.where(position < from_upper, width, 2 * width))
@@ -646,7 +689,7 @@
             item_left[count] = (column - base) * splits + part
             item_index[count] = index
             item_seat[count] = jnp.where(column == away, -1 - other_seat, other_seat)
-            count = count + valid * (counts[column] > part * ROWS).astype(jnp.int32)
+            count = count + valid * (count_of(column) > part * ROWS).astype(jnp.int32)
 
         far = local[other] + displacement(step_x, step_y, wrap)
         row = lax.broadcasted_iota(jnp.int32, (8, LEAF), 0)
@@ -674,17 +717,25 @@
 
     mine[kept] = mine[0]
     item_count = lax.fori_loop(0, (kept + 1) // 2, prepare_two, 0)
-    item_left[item_count] = 0
-    item_index[item_count] = 0
-
-    def forms(position):
+    for extra in range(2):
+        item_left[item_count + extra] = 0
+        item_index[item_count + extra] = 0
+
+    def state_forms(position):
         index = item_index[position]
         left = item_left[position]
         near_form[...] = jnp.dot(
-            near_left[left, :, 0:48], near_right[index], preferred_element_type=F32
+            near_left[left, ROWS : 6 * ROWS, 0:48], near_right[index], preferred_element_type=F32
         )
         far_form[...] = jnp.dot(
             far_left[left, :, 0:48], far_right[index], preferred_element_type=F32
+        )
+
+    def space_forms(position):
+        index = item_index[position]
+        left = item_left[position]
+        dist_form[...] = jnp.dot(
+            near_left[left, 0:ROWS, 0:48], near_right[index], preferred_element_type=F32
         )
         for k in range(3):
             toward_form[k * ROWS : (k + 1) * ROWS, :] = jnp.dot(
@@ -692,6 +743,15 @@
                 toward_right[index, :, k * LEAF : (k + 1) * LEAF],
                 preferred_element_type=F32,
             )
+
+    def geometry():
+        return face_geometry(
+            dist_form[...], [toward_form[k * ROWS : (k + 1) * ROWS, :] for k in range(3)]
+        )
+
+    def keep_geometry(values):
+        for k in range(4):
+            geo_form[k * ROWS : (k + 1) * ROWS, :] = values[k]
 
     def flux_item(position, carry):
         left = item_left[position]
@@ -700,13 +760,17 @@
         other_seat = jnp.where(coded < 0, -1 - coded, coded)
         weight = jnp.where(coded < 0, 0.0, 1.0).astype(F32)
         fluxes = face_fluxes(
-            [near_form[k * ROWS : (k + 1) * ROWS, :] for k in range(6)],
+            [near_form[k * ROWS : (k + 1) * ROWS, :] for k in range(5)],
             [far_form[:, k * LEAF : (k + 1) * LEAF] for k in range(5)],
-            [toward_form[k * ROWS : (k + 1) * ROWS, :] for k in range(3)],
+            [geo_form[k * ROWS : (k + 1) * ROWS, :] for k in range(3)],
+            geo_form[3 * ROWS : 4 * ROWS, :],
             [near_plane[left, k] for k in range(5)],
             [far_half[index, k : k + 1, :] for k in range(5)],
         )
-        forms(position + 1)
+        following = geometry()
+        keep_geometry(following)
+        state_forms(position + 1)
+        space_forms(position + 2)
         for k in range(5):
             row_sum[left, k] += fluxes[k]
             col_sum[other_seat, 8 * k : 8 * k + 8] += weight * sum(
@@ -714,7 +778,10 @@
             )
         return carry
 
-    forms(0)
+    space_forms(0)
+    keep_geometry(geometry())
+    state_forms(0)
+    space_forms(1)
     lax.fori_loop(0, item_count, flux_item, 0)
 
     lane = lax.broadcasted_iota(jnp.int32, (ROWS, LEAF), 1)
@@ -772,25 +839,29 @@
 
     smem = pl.BlockSpec(memory_space=pltpu.SMEM)
     vmem = pl.BlockSpec(memory_space=pltpu.VMEM)
-    lanes = -(-(slots + leaf_sub + 1) // LEAF) * LEAF
+    lanes = -(-(slots + max(leaf_sub + 1, width)) // LEAF) * LEAF
     state, listed = pl.pallas_call(
         functools.partial(pack_kernel, width, leaf_sub),
         out_shape=[
             jax.ShapeDtypeStruct((8, particles), F32),
             jax.ShapeDtypeStruct((4, lanes), F32),
         ],
-        in_specs=[smem, vmem, vmem, vmem, vmem, vmem],
+        in_specs=[smem, vmem, vmem, vmem, vmem, vmem, vmem],
         out_specs=[vmem, vmem],
         name="pack",
     )(
         counts,
+        counts[None],
         positions,
         velocity,
         density[None],
         pressure[None],
         pair_list,
     )
-    lists = jnp.stack([shifted(listed, "slab", 1), listed, shifted(listed, "slab", -1)])[None]
+    kept_state, kept_listed = lax.optimization_barrier(
+        (jnp.where(state == state, state, 0.0), jnp.where(listed == listed, listed, 0.0))
+    )
+    lists = jnp.stack([shifted(listed, "slab", 1), kept_listed, shifted(listed, "slab", -1)])[None]
     lower = shifted(state, "slab", 1)
     upper = shifted(state, "slab", -1)
     beyond = shifted(state, "slab", -2)
@@ -806,7 +877,7 @@
     own_part, next_part = pl.pallas_call(
         functools.partial(step_kernel, width, sub_count, slots),
         out_shape=[jax.ShapeDtypeStruct((5 * width, LEAF), F32)] * 2,
-        in_specs=[smem, smem, vmem, vmem, vmem, vmem],
+        in_specs=[smem, vmem, vmem, vmem, vmem],
         out_specs=[vmem, vmem],
         scratch_shapes=[
             pltpu.SMEM((3 * sub_count * slots + 2 * UNROLL,), jnp.int32),
@@ -814,7 +885,7 @@
             pltpu.SMEM((7 * width + 1,), jnp.int32),
             pltpu.SMEM((width,), jnp.int32),
         ]
-        + [pltpu.SMEM((most * splits + 1,), jnp.int32)] * 3
+        + [pltpu.SMEM((most * splits + 2,), jnp.int32)] * 3
         + [
             pltpu.VMEM((4 * width + 1, 8, LEAF), F32),
             pltpu.VMEM((4 * width + 1, 32, LEAF), F32),
@@ -830,16 +901,18 @@
             pltpu.VMEM((most, 8, LEAF), F32),
             pltpu.VMEM((48, 5 * LEAF), BF16),
             pltpu.VMEM((UNROLL, LEAF, LEAF), F32),
-            pltpu.VMEM((6 * ROWS, LEAF), F32),
+            pltpu.VMEM((5 * ROWS, LEAF), F32),
             pltpu.VMEM((ROWS, 5 * LEAF), F32),
             pltpu.VMEM((3 * ROWS, LEAF), F32),
+            pltpu.VMEM((ROWS, LEAF), F32),
+            pltpu.VMEM((4 * ROWS, LEAF), F32),
             pltpu.VMEM((2 * cap + 3, 40, LEAF), F32),
             pltpu.VMEM((cap * splits, 5, ROWS, LEAF), F32),
             pltpu.VMEM((cap + 1, 8, LEAF), F32),
         ],
         compiler_params=pltpu.CompilerParams(vmem_limit_bytes=48 * 1024 * 1024),
         name="hydro_step",
-    )(rec, counts, lower, state, upper, beyond)
+    )(rec, lower, kept_state, upper, beyond)
 
     merged = own_part + shifted(next_part, "slab", 1)
     mask = 1

time: 71.2 us -> 63.6 us (0.89)
  Pallas kernels: 33.9 us -> 27.7 us
  local copies, waits for them, and re-layouts: 2.75 us -> 0.68 us
  waiting for transfers between devices: 17.3 us -> 16 us
  other arithmetic: 0.05 us -> 1.04 us
  starting transfers between devices: 17.9 us -> 18.7 us
    pallas_call x1, Pallas kernels: 32 us -> 25.8 us  [shards(): pl.pallas_call(functools.partial(step_kernel, width, sub_count, slots), o...]
    unnamed x6 -> x4, local copies, waits for them, and re-layouts: 2.08 us -> 0.01 us
    ppermute x6, starting transfers between devices: 7.44 us -> 9.03 us  [shifted(): lax.ppermute(shard, axis, [(i, (i + by) % peers) for i in range(peers)])]
    ppermute x4, waiting for transfers between devices: 11.9 us -> 10.6 us  [swapped(): return lax.ppermute(shard, axis, [(i, i ^ mask) for i in range(peers)])]
    select_n x0 -> x2, other arithmetic: none -> 0.99 us  [the longest x1 0.99 us: shards(): jnp.where(state == state, state, 0.0)]
    ppermute x4, starting transfers between devices: 10.5 us -> 9.67 us  [swapped(): return lax.ppermute(shard, axis, [(i, i ^ mask) for i in range(peers)])]
  transfers between devices with their start and end apart: 10 -> 10, of which waited for: 8 -> 8; matrix products, arithmetic and copies ran while one was open for 0% -> 2% of each run, Pallas kernels for 0% -> 0%
where the time goes in v1:
time: 63.6 us; the launch traced here: 64.1 us
  Pallas kernels  27.7 us (44%)
  starting transfers between devices  18.7 us (29%)
  waiting for transfers between devices  16 us (25%)
  other arithmetic  1.04 us (2%)
  local copies, waits for them, and re-layouts  0.68 us (1%)
    pallas_call x1, Pallas kernels, shards(): pl.pallas_call(functools.partial(step_kernel, width, sub_count, slots), o...  25.8 us
    ppermute x4, waiting for transfers between devices, swapped(): return lax.ppermute(shard, axis, [(i, i ^ mask) for i in range(peers)])  10.6 us
    ppermute x4, starting transfers between devices, swapped(): return lax.ppermute(shard, axis, [(i, i ^ mask) for i in range(peers)])  9.67 us
    ppermute x6, starting transfers between devices, shifted(): lax.ppermute(shard, axis, [(i, (i + by) % peers) for i in range(peers)])  9.03 us
    ppermute x6, waiting for transfers between devices, shifted(): lax.ppermute(shard, axis, [(i, (i + by) % peers) for i in range(peers)])  5.41 us
    pallas_call x1, Pallas kernels, shards(): pl.pallas_call(functools.partial(pack_kernel, width, leaf_sub), out_shape...  1.88 us
  transfers between devices with their start and end apart: 10, of which 8 were waited for; matrix products, arithmetic and copies ran while one was open for 2% of the time, Pallas kernels for 0%

profile of v1, /device:TPU:0, one launch (start us, length us, event | category | flops | bytes accessed | tf_op | source)
XLA Modules:
  0.0 64.1 jit_solution(13354058685337447943)
XLA Ops:
  0.0 1.9 %pack.1 = (f32[8,4096]{1,0:T(8,128)}, f32[4,128]{1,0:T(4,128)}) custom-call(s32[32]{0:T(128)} %counts.1, s32[1,32]{1,0:T(1,128)} %bitcast.13, f32[3,4096]{1,0:T(4,128)} %positions.1, f32[3,4096]{1,0:T(4,128)} %velocity.1, f32[1,4096]{1,0:T(1,128)} %bitcast.10, f32[1,4096]{1,0:T(1,128)} %bitcast.11, s32[3,40]{1,0:T(4,128)} %pair_list.1), custom_call_target="tpu_custom_call" | custom-call | tf_op jit(solution)/shard_map/pack/pallas_call | solution.py:843
  1.9 3.3 %collective-permute-start.1 = (f32[4,128]{1,0:T(4,128)}, f32[4,128]{1,0:T(4,128)S(1)}, u32[]{:S(2)}, u32[]{:S(2)}) collective-permute-start(f32[4,128]{1,0:T(4,128)} %get-tuple-element.11), channel_id=1, source_target_pairs={{0,28},{4,0},{8,4},{12,8},{16,12},{20,16},{24,20},{28,24},{1,29},{... | collective-permute-start | bytes 6152 | tf_op jit(solution)/shard_map/ppermute | solution.py:30
  5.2 0.0 collective-permute-start
  5.2 0.0 copy-start.1
  5.2 0.0 copy-start
  5.2 1.0 %compare_select_fusion.own_ref = f32[8,4096]{1,0:T(8,128)S(1)} fusion(f32[8,4096]{1,0:T(8,128)} %get-tuple-element.12), kind=kLoop, calls=%fused_computation | loop fusion | flops 65536 | bytes 262144 | tf_op jit(solution)/shard_map/jit(_where)/select_n | solution.py:862
  6.2 0.0 copy-done.1
  6.2 0.5 collective-permute-done.1
  6.7 2.6 %collective-permute-done = f32[4,128]{1,0:T(4,128)S(1)} collective-permute-done((f32[4,128]{1,0:T(4,128)}, f32[4,128]{1,0:T(4,128)S(1)}, u32[]{:S(2)}, u32[]{:S(2)}) %collective-permute-start) | collective-permute-done | bytes 2080 | tf_op jit(solution)/shard_map/ppermute | solution.py:30
  9.3 1.6 %collective-permute-start.2 = (f32[1,3,4,128]{3,2,1,0:T(4,128)S(1)}, f32[1,3,4,128]{3,2,1,0:T(4,128)S(1)}, u32[]{:S(2)}, u32[]{:S(2)}) collective-permute-start(f32[1,3,4,128]{3,2,1,0:T(4,128)S(1)} %maximum_bitcast_fusion), channel_id=1, source_target_pairs={{0,1},{1,0},{2,3},{3,2},{4,5},{5,4},{6,7},{7,6},{8,9},{9,8},{10,11... | collective-permute-start | bytes 18440 | tf_op jit(solution)/shard_map/ppermute | solution.py:35
  10.9 0.0 copy-done
  10.9 0.0 collective-permute-start.5
  10.9 0.5 collective-permute-start.4
  11.4 0.0 collective-permute-start.6
  11.4 1.5 %collective-permute-done.2 = f32[1,3,4,128]{3,2,1,0:T(4,128)S(1)} collective-permute-done((f32[1,3,4,128]{3,2,1,0:T(4,128)S(1)}, f32[1,3,4,128]{3,2,1,0:T(4,128)S(1)}, u32[]{:S(2)}, u32[]{:S(2)}) %collective-permute-start.2) | collective-permute-done | bytes 6176 | tf_op jit(solution)/shard_map/ppermute | solution.py:35
  13.0 2.6 %collective-permute-start.3 = (f32[2,3,4,128]{3,2,1,0:T(4,128)S(1)}, f32[2,3,4,128]{3,2,1,0:T(4,128)S(1)}, u32[]{:S(2)}, u32[]{:S(2)}) collective-permute-start(f32[2,3,4,128]{3,2,1,0:T(4,128)S(1)} %pad_maximum_fusion), channel_id=1, source_target_pairs={{0,2},{1,3},{2,0},{3,1},{4,6},{5,7},{6,4},{7,5},{8,10},{9,11},{10,... | collective-permute-start | bytes 36872 | tf_op jit(solution)/shard_map/ppermute | solution.py:35
  15.6 2.0 %collective-permute-done.3 = f32[2,3,4,128]{3,2,1,0:T(4,128)S(1)} collective-permute-done((f32[2,3,4,128]{3,2,1,0:T(4,128)S(1)}, f32[2,3,4,128]{3,2,1,0:T(4,128)S(1)}, u32[]{:S(2)}, u32[]{:S(2)}) %collective-permute-start.3) | collective-permute-done | bytes 12320 | tf_op jit(solution)/shard_map/ppermute | solution.py:35
  17.6 0.0 collective-permute-done.5.upper_ref
  17.6 0.0 collective-permute-done.4.lower_ref
  17.6 0.2 collective-permute-done.6.beyond_ref
  17.8 25.8 %hydro_step.1 = (f32[160,128]{1,0:T(8,128)S(1)}, f32[160,128]{1,0:T(8,128)S(1)}) custom-call(s32[6144]{0:T(1024)S(1)} %bitcast.9, f32[8,4096]{1,0:T(8,128)S(1)} %collective-permute-done.4.lower_ref, f32[8,4096]{1,0:T(8,128)S(1)} %compare_select_fusion.own_ref, f32[8,4096]{1,0:T(8,128)S(1)} %collective-permute-done.5.upper_ref, ...), custom_call_target="tpu_custom_call" | custom-call | tf_op jit(solution)/shard_map/hydro_step/pallas_call | solution.py:877
  43.6 5.2 %collective-permute-start.7 = (f32[160,128]{1,0:T(8,128)S(1)}, f32[160,128]{1,0:T(8,128)S(1)}, u32[]{:S(2)}, u32[]{:S(2)}) collective-permute-start(f32[160,128]{1,0:T(8,128)S(1)} %get-tuple-element.16), channel_id=1, source_target_pairs={{0,4},{4,8},{8,12},{12,16},{16,20},{20,24},{24,28},{28,0},{1,5},{5... | collective-permute-start | bytes 245768 | tf_op jit(solution)/shard_map/ppermute | solution.py:30
  48.8 2.1 %collective-permute-done.7 = f32[160,128]{1,0:T(8,128)S(1)} collective-permute-done((f32[160,128]{1,0:T(8,128)S(1)}, f32[160,128]{1,0:T(8,128)S(1)}, u32[]{:S(2)}, u32[]{:S(2)}) %collective-permute-start.7) | collective-permute-done | bytes 81952 | tf_op jit(solution)/shard_map/ppermute | solution.py:30
  50.9 4.7 %collective-permute-start.8 = (f32[160,128]{1,0:T(8,128)S(1)}, f32[160,128]{1,0:T(8,128)S(1)}, u32[]{:S(2)}, u32[]{:S(2)}) collective-permute-start(f32[160,128]{1,0:T(8,128)S(1)} %add.9), channel_id=1, source_target_pairs={{0,1},{1,0},{2,3},{3,2},{4,5},{5,4},{6,7},{7,6},{8,9},{9,8},{10,11... | collective-permute-start | bytes 245768 | tf_op jit(solution)/shard_map/ppermute | solution.py:35
  55.6 2.4 %collective-permute-done.8 = f32[160,128]{1,0:T(8,128)S(1)} collective-permute-done((f32[160,128]{1,0:T(8,128)S(1)}, f32[160,128]{1,0:T(8,128)S(1)}, u32[]{:S(2)}, u32[]{:S(2)}) %collective-permute-start.8) | collective-permute-done | bytes 81952 | tf_op jit(solution)/shard_map/ppermute | solution.py:35
  58.1 0.8 %collective-permute-start.9 = (f32[160,128]{1,0:T(8,128)S(1)}, f32[160,128]{1,0:T(8,128)S(1)}, u32[]{:S(2)}, u32[]{:S(2)}) collective-permute-start(f32[160,128]{1,0:T(8,128)S(1)} %add.10), channel_id=1, source_target_pairs={{0,2},{1,3},{2,0},{3,1},{4,6},{5,7},{6,4},{7,5},{8,10},{9,11},{10,... | collective-permute-start | bytes 245768 | tf_op jit(solution)/shard_map/ppermute | solution.py:35
  58.8 4.6 %collective-permute-done.9 = f32[160,128]{1,0:T(8,128)S(1)} collective-permute-done((f32[160,128]{1,0:T(8,128)S(1)}, f32[160,128]{1,0:T(8,128)S(1)}, u32[]{:S(2)}, u32[]{:S(2)}) %collective-permute-start.9) | collective-permute-done | bytes 81952 | tf_op jit(solution)/shard_map/ppermute | solution.py:35
  63.5 0.7 %reshape.6 = f32[5,4096]{1,0:T(8,128)} reshape(f32[160,128]{1,0:T(8,128)S(1)} %add.11) | data formatting | bytes 163840 | tf_op jit(solution)/shard_map/reshape | solution.py:922
  (7 shorter events, 0.1 us)
Async XLA Ops:
  1.9 4.9 %collective-permute-start.1 = (f32[4,128]{1,0:T(4,128)}, f32[4,128]{1,0:T(4,128)S(1)}, u32[]{:S(2)}, u32[]{:S(2)}) collective-permute-start(f32[4,128]{1,0:T(4,128)} %get-tuple-element.11), channel_id=1, source_target_pairs={{0,28},{4,0},{8,4},{12,8},{16,12},{20,16},{24,20},{28,24},{1,29},{... | collective-permute-start | bytes 6152 | tf_op jit(solution)/shard_map/ppermute | solution.py:30
  5.2 4.1 %collective-permute-start = (f32[4,128]{1,0:T(4,128)}, f32[4,128]{1,0:T(4,128)S(1)}, u32[]{:S(2)}, u32[]{:S(2)}) collective-permute-start(f32[4,128]{1,0:T(4,128)} %get-tuple-element.11), channel_id=1, source_target_pairs={{0,4},{4,8},{8,12},{12,16},{16,20},{20,24},{24,28},{28,0},{1,5},{5... | collective-permute-start | bytes 6152 | tf_op jit(solution)/shard_map/ppermute | solution.py:30
  5.2 1.0 %copy-start.1 = (f32[4,128]{1,0:T(4,128)S(1)}, f32[4,128]{1,0:T(4,128)}, u32[]{:S(2)}) copy-start(f32[4,128]{1,0:T(4,128)} %get-tuple-element.11) | copy-start | bytes 6148
  5.2 5.7 %copy-start = (f32[8,4096]{1,0:T(8,128)S(1)}, f32[8,4096]{1,0:T(8,128)}, u32[]{:S(2)}) copy-start(f32[8,4096]{1,0:T(8,128)} %get-tuple-element.12) | copy-start | bytes 393220
  9.3 3.6 %collective-permute-start.2 = (f32[1,3,4,128]{3,2,1,0:T(4,128)S(1)}, f32[1,3,4,128]{3,2,1,0:T(4,128)S(1)}, u32[]{:S(2)}, u32[]{:S(2)}) collective-permute-start(f32[1,3,4,128]{3,2,1,0:T(4,128)S(1)} %maximum_bitcast_fusion), channel_id=1, source_target_pairs={{0,1},{1,0},{2,3},{3,2},{4,5},{5,4},{6,7},{7,6},{8,9},{9,8},{10,11... | collective-permute-start | bytes 18440 | tf_op jit(solution)/shard_map/ppermute | solution.py:35
  10.9 6.7 %collective-permute-start.5 = (f32[8,4096]{1,0:T(8,128)S(1)}, f32[8,4096]{1,0:T(8,128)S(1)}, u32[]{:S(2)}, u32[]{:S(2)}) collective-permute-start(f32[8,4096]{1,0:T(8,128)S(1)} %copy-done), channel_id=1, source_target_pairs={{0,28},{4,0},{8,4},{12,8},{16,12},{20,16},{24,20},{28,24},{1,29},{... | collective-permute-start | bytes 393224 | tf_op jit(solution)/shard_map/ppermute | solution.py:30
  10.9 6.7 %collective-permute-start.4 = (f32[8,4096]{1,0:T(8,128)S(1)}, f32[8,4096]{1,0:T(8,128)S(1)}, u32[]{:S(2)}, u32[]{:S(2)}) collective-permute-start(f32[8,4096]{1,0:T(8,128)S(1)} %copy-done), channel_id=1, source_target_pairs={{0,4},{4,8},{8,12},{12,16},{16,20},{20,24},{24,28},{28,0},{1,5},{5... | collective-permute-start | bytes 393224 | tf_op jit(solution)/shard_map/ppermute | solution.py:30
  11.4 6.4 %collective-permute-start.6 = (f32[8,4096]{1,0:T(8,128)S(1)}, f32[8,4096]{1,0:T(8,128)S(1)}, u32[]{:S(2)}, u32[]{:S(2)}) collective-permute-start(f32[8,4096]{1,0:T(8,128)S(1)} %copy-done), channel_id=1, source_target_pairs={{0,24},{4,28},{8,0},{12,4},{16,8},{20,12},{24,16},{28,20},{1,25},{... | collective-permute-start | bytes 393224 | tf_op jit(solution)/shard_map/ppermute | solution.py:30
  13.0 4.6 %collective-permute-start.3 = (f32[2,3,4,128]{3,2,1,0:T(4,128)S(1)}, f32[2,3,4,128]{3,2,1,0:T(4,128)S(1)}, u32[]{:S(2)}, u32[]{:S(2)}) collective-permute-start(f32[2,3,4,128]{3,2,1,0:T(4,128)S(1)} %pad_maximum_fusion), channel_id=1, source_target_pairs={{0,2},{1,3},{2,0},{3,1},{4,6},{5,7},{6,4},{7,5},{8,10},{9,11},{10,... | collective-permute-start | bytes 36872 | tf_op jit(solution)/shard_map/ppermute | solution.py:35
  43.6 7.3 %collective-permute-start.7 = (f32[160,128]{1,0:T(8,128)S(1)}, f32[160,128]{1,0:T(8,128)S(1)}, u32[]{:S(2)}, u32[]{:S(2)}) collective-permute-start(f32[160,128]{1,0:T(8,128)S(1)} %get-tuple-element.16), channel_id=1, source_target_pairs={{0,4},{4,8},{8,12},{12,16},{16,20},{20,24},{24,28},{28,0},{1,5},{5... | collective-permute-start | bytes 245768 | tf_op jit(solution)/shard_map/ppermute | solution.py:30
  50.9 7.1 %collective-permute-start.8 = (f32[160,128]{1,0:T(8,128)S(1)}, f32[160,128]{1,0:T(8,128)S(1)}, u32[]{:S(2)}, u32[]{:S(2)}) collective-permute-start(f32[160,128]{1,0:T(8,128)S(1)} %add.9), channel_id=1, source_target_pairs={{0,1},{1,0},{2,3},{3,2},{4,5},{5,4},{6,7},{7,6},{8,9},{9,8},{10,11... | collective-permute-start | bytes 245768 | tf_op jit(solution)/shard_map/ppermute | solution.py:35
  58.1 5.4 %collective-permute-start.9 = (f32[160,128]{1,0:T(8,128)S(1)}, f32[160,128]{1,0:T(8,128)S(1)}, u32[]{:S(2)}, u32[]{:S(2)}) collective-permute-start(f32[160,128]{1,0:T(8,128)S(1)} %add.10), channel_id=1, source_target_pairs={{0,2},{1,3},{2,0},{3,1},{4,6},{5,7},{6,4},{7,5},{8,10},{9,11},{10,... | collective-permute-start | bytes 245768 | tf_op jit(solution)/shard_map/ppermute | solution.py:35

commit v2 on v1

--- a/solution.py
+++ b/solution.py
@@ -93,15 +93,15 @@
     return jnp.where(row == 4, -wrap, out)
 
 
-def finish_leaf(raw, tile):
-    pos = [tile[k : k + 1] for k in range(3)]
+def finish_leaves(raw, tile):
+    pos = [tile(k) for k in range(3)]
     live = pos[0] < 0.5 * AWAY
-    total = raw[16:17]
-    first = [raw[k : k + 1] - pos[k] * total for k in range(3)]
+    total = raw(16)
+    first = [raw(k) - pos[k] * total for k in range(3)]
 
     def second(left, right):
-        lead = raw[8 + 8 * left + right : 9 + 8 * left + right]
-        return lead - pos[left] * raw[right : right + 1] - pos[right] * first[left]
+        lead = raw(8 + 8 * left + right)
+        return lead - pos[left] * raw(right) - pos[right] * first[left]
 
     density = jnp.where(live, total, 1.0)
     inverse_density = 1.0 / density
@@ -126,11 +126,11 @@
     square = inverse_density * inverse_density
     rows = [density] + [entry * square for entry in inverse]
     for quantity in range(3, 8):
-        value = tile[quantity : quantity + 1]
+        value = tile(quantity)
         along = [
             scaled(
-                raw[8 + 8 * k + quantity : 9 + 8 * k + quantity]
-                - pos[k] * raw[quantity : quantity + 1]
+                raw(8 + 8 * k + quantity)
+                - pos[k] * raw(quantity)
                 - value * first[k]
             )
             for k in range(3)
@@ -139,8 +139,7 @@
         rows.append(inverse[0] * half[0] + inverse[1] * half[1] + inverse[2] * half[2])
         rows.append(inverse[1] * half[0] + inverse[3] * half[1] + inverse[4] * half[2])
         rows.append(inverse[2] * half[0] + inverse[4] * half[1] + inverse[5] * half[2])
-    rows.append(jnp.zeros((2, LEAF), F32))
-    return jnp.concatenate(rows, axis=0)
+    return rows
 
 
 def dot3(left, right):
@@ -192,22 +191,22 @@
 
 
 def far_coefficients(tile, pay):
-    pos = [tile[k : k + 1] for k in range(3)]
+    pos = [tile(k) for k in range(3)]
     out = []
-    matrix = [pay[1 + k : 2 + k] for k in range(6)]
+    matrix = [pay[1 + k] for k in range(6)]
     for line in ((0, 1, 2), (1, 3, 4), (2, 4, 5)):
         entries = [matrix[k] for k in line]
         out.append({0: dot3(entries, pos), 1: -entries[0], 2: -entries[1], 3: -entries[2]})
     for quantity in range(5):
-        slope = [pay[7 + 3 * quantity + k : 8 + 3 * quantity + k] for k in range(3)]
-        value = tile[3 + quantity : 4 + quantity]
+        slope = [pay[7 + 3 * quantity + k] for k in range(3)]
+        value = tile(3 + quantity)
         if quantity < 3:
             entry = {0: 0.5 * value - dot3(slope, pos), 4 + quantity: -0.5}
         else:
             entry = {0: value - dot3(slope, pos)}
         entry.update({1: slope[0], 2: slope[1], 3: slope[2]})
         out.append(entry)
-    return [stack_rows(entry) for entry in out]
+    return out
 
 
 def limited(value, low, high):
@@ -333,6 +332,10 @@
     listed[3:4, slots : slots + leaf_sub + 1] = facts
 
 
+def upper_seat_of(cap):
+    return -(-(cap + 2) // 8) * 8
+
+
 def step_kernel(
     width,
     sub_count,
@@ -351,6 +354,7 @@
     item_left,
     item_index,
     item_seat,
+    turned_leaf,
     local,
     raw,
     pay,
@@ -377,6 +381,7 @@
     whole = 4 * width
     leaf_sub = width // sub_count
     cap = 2 * leaf_sub
+    up = upper_seat_of(cap)
     stride = rec.shape[0] // (12 * sub_count)
     block = 4 * stride
 
@@ -517,23 +522,32 @@
     for extra in range(2 * UNROLL):
         order[used + extra] = -1
 
+    def rows_of(leaf, count):
+        return pl.ds(pl.multiple_of(leaf * count, count), count)
+
     def load_leaf(column, carry):
         lanes = pl.ds(pl.multiple_of(column * LEAF, LEAF), LEAF)
-        local[column] = lower_ref[:, lanes]
-        local[width + column] = own_ref[:, lanes]
-        local[2 * width + column] = upper_ref[:, lanes]
-        local[3 * width + column] = beyond_ref[:, lanes]
+        places = (
+            column,
+            width + lax.rem(column - base + width, width),
+            2 * width + lax.rem(column - upper_base + width, width),
+            3 * width + column,
+        )
+        for slab, ref in enumerate((lower_ref, own_ref, upper_ref, beyond_ref)):
+            local[rows_of(places[slab], 8), :] = ref[:, lanes]
+            turned_leaf[slab * width + column] = places[slab]
+            raw[rows_of(slab * width + column, 32), :] = jnp.zeros((32, LEAF), F32)
         for k in range(5):
             own_out[pl.ds(k * width + column, 1), :] = jnp.zeros((1, LEAF), F32)
             next_out[pl.ds(k * width + column, 1), :] = jnp.zeros((1, LEAF), F32)
-        for slab in range(4):
-            raw[slab * width + column] = jnp.zeros((32, LEAF), F32)
         return carry
 
     lax.fori_loop(0, width, load_leaf, 0)
-    local[whole] = jnp.zeros((8, LEAF), F32)
-    raw[whole] = jnp.zeros((32, LEAF), F32)
-
+    local[rows_of(whole, 8), :] = jnp.zeros((8, LEAF), F32)
+    raw[rows_of(whole, 32), :] = jnp.zeros((32, LEAF), F32)
+
+    def tile_of(leaf):
+        return local[rows_of(leaf, 8), :]
 
     def slab_base(position):
         return jnp.where(position < from_own, 0, jnp.where(position < from_upper, width, 2 * width))
@@ -551,7 +565,7 @@
         return carry
 
     lax.fori_loop(0, length + 1, clear_cols, 0)
-    lax.fori_loop(cap + 1, cap + length + 3, clear_cols, 0)
+    lax.fori_loop(up, up + length + 2, clear_cols, 0)
 
     def slot_tiles(position):
         named = order[position]
@@ -561,9 +575,9 @@
         shift = displacement(
             jnp.where(other >= width, 1.0, 0.0).astype(F32), slot_step_y(slot), slot_wrap(slot)
         )
-        home = jnp.where(named < 0, whole, start + slot_home(slot))
-        other = jnp.where(named < 0, whole, start + other)
-        return home, other, local[home], local[other] + shift, shift
+        home = jnp.where(named < 0, whole, turned_leaf[jnp.where(named < 0, 0, start + slot_home(slot))])
+        other = jnp.where(named < 0, whole, turned_leaf[jnp.where(named < 0, 0, start + other)])
+        return home, other, tile_of(home), tile_of(other) + shift, shift
 
     def distances(group):
         row = lax.broadcasted_iota(jnp.int32, (8, LEAF), 0)
@@ -610,26 +624,35 @@
             parts.append((home, other, row_part, col_part))
         distances(group + 1)
         for home, other, row_part, col_part in parts:
-            raw[home] += row_part[:32] + row_part[32:]
-            raw[other] += col_part[:32] + col_part[32:]
+            raw[rows_of(home, 32), :] += row_part[:32] + row_part[32:]
+            raw[rows_of(other, 32), :] += col_part[:32] + col_part[32:]
         return carry
 
     distances(0)
     lax.fori_loop(0, (used + UNROLL - 1) // UNROLL, moment_group, 0)
 
-    def window_leaf(seat):
-        return jnp.where(seat <= cap, own_leaf(seat), upper_leaf(seat - cap - 1))
-
-    def finish(seat, carry):
-        leaf = window_leaf(seat)
-        payload = finish_leaf(raw[leaf], local[leaf])
-        pay[seat] = payload
-        for k, entry in enumerate(far_coefficients(local[leaf], payload)):
-            far_coef[seat, 8 * k : 8 * k + 8] = entry
-        return carry
-
-    lax.fori_loop(0, length + 1, finish, 0)
-    lax.fori_loop(cap + 1, cap + length + 3, finish, 0)
+    def finish(first_leaf, first_seat):
+        def tile(k):
+            return local[pl.ds(first_leaf * 8 + k, 8, stride=8), :]
+
+        payload = finish_leaves(lambda k: raw[pl.ds(first_leaf * 32 + k, 8, stride=32), :], tile)
+        for k, entry in enumerate(payload):
+            pay[pl.ds(first_seat * 24 + k, 8, stride=24), :] = entry
+        for k, entry in enumerate(far_coefficients(tile, payload)):
+            for row in range(8):
+                value = jnp.broadcast_to(jnp.asarray(entry.get(row, 0.0), F32), (8, LEAF))
+                far_coef[pl.ds(first_seat * 64 + 8 * k + row, 8, stride=64), :] = value
+
+    def finish_own(group, carry):
+        finish(width + 8 * group, 8 * group)
+        return carry
+
+    def finish_upper(group, carry):
+        finish(2 * width + 8 * group, up + 8 * group)
+        return carry
+
+    lax.fori_loop(0, (length + 8) // 8, finish_own, 0)
+    lax.fori_loop(0, (length + 9) // 8, finish_upper, 0)
 
     splits = LEAF // ROWS
 
@@ -641,11 +664,12 @@
         )
 
     def turn_home(seat):
-        tile = local[own_leaf(seat)]
+        tile = tile_of(width + seat)
+        payload = pay[rows_of(seat, 24), :]
         generic = {0: 1.0}
         generic.update({1 + k: tile[k : k + 1] for k in range(6)})
         generic = stack_near(stack_rows(generic))
-        coefficients = [stack_near(entry) for entry in near_coefficients(tile, pay[seat])]
+        coefficients = [stack_near(entry) for entry in near_coefficients(tile, payload)]
         planes = jnp.dot(stack_near(tile).T, spread[...], preferred_element_type=F32)
         turned_far = generic.T
         turned_near = [coefficients[k].T for k in (0, 4, 5, 6, 7, 8)]
@@ -682,7 +706,7 @@
         wrap = slot_wrap(slot)
         other_seat = jnp.where(
             is_upper,
-            cap + 1 + lax.rem(away - upper_base, width),
+            up + lax.rem(away - upper_base, width),
             lax.rem(away + width - base, width),
         )
         for part in range(splits):
@@ -691,7 +715,7 @@
             item_seat[count] = jnp.where(column == away, -1 - other_seat, other_seat)
             count = count + valid * (count_of(column) > part * ROWS).astype(jnp.int32)
 
-        far = local[other] + displacement(step_x, step_y, wrap)
+        far = tile_of(turned_leaf[other]) + displacement(step_x, step_y, wrap)
         row = lax.broadcasted_iota(jnp.int32, (8, LEAF), 0)
         pos = [far[k : k + 1] for k in range(3)]
         generic = {0: 1.0, 7: dot3(pos, pos)}
@@ -699,7 +723,7 @@
         generic = stack_far(stack_rows(generic))
         near_right[index] = generic
         for k in range(8):
-            entry = far_coef[other_seat, 8 * k : 8 * k + 8]
+            entry = far_coef[pl.ds(pl.multiple_of(other_seat * 64 + 8 * k, 8), 8), :]
             change = entry[1:2] * step_x + entry[2:3] * step_y
             if k == 4:
                 change = change + 0.5 * wrap
@@ -784,24 +808,19 @@
     space_forms(1)
     lax.fori_loop(0, item_count, flux_item, 0)
 
-    lane = lax.broadcasted_iota(jnp.int32, (ROWS, LEAF), 1)
-
     def row_total(seat, carry):
-        pieces = []
-        for part in range(splits):
-            total = jnp.zeros((ROWS, LEAF), F32)
-            for c in range(5):
-                reduced = jnp.sum(row_sum[seat * splits + part, c], axis=1, keepdims=True)
-                total = jnp.where(lane == c, reduced, total)
-            pieces.append(total)
-        row_rate[seat] = jnp.concatenate(pieces, axis=0).T[0:8]
+        sums = {}
+        for c in range(5):
+            pieces = [row_sum[seat * splits + part, c] for part in range(splits)]
+            turned = jnp.concatenate(pieces, axis=0).T
+            sums[c] = jnp.sum(turned, axis=0, keepdims=True)
+        row_rate[seat] = stack_rows(sums)
         return carry
 
     lax.fori_loop(0, length, row_total, 0)
     row_rate[length] = jnp.zeros((8, LEAF), F32)
 
-    def rates(seat, less):
-        leaf = window_leaf(seat)
+    def rates(seat, less, leaf, column):
         total = stack_rows(
             {
                 k: jnp.sum(col_sum[seat, 8 * k : 8 * k + 8], axis=0, keepdims=True)
@@ -810,24 +829,24 @@
         )
         if less is not None:
             total = total - less
-        live = local[leaf][0:1] < 0.5 * AWAY
-        scale = AREA_FLOOR * pay[seat][0:1]
-        return lax.rem(leaf, width), jnp.where(live, total * scale, 0.0)
+        live = tile_of(leaf)[0:1] < 0.5 * AWAY
+        scale = AREA_FLOOR * pay[rows_of(seat, 24), :][0:1]
+        return lax.rem(column, width), jnp.where(live, total * scale, 0.0)
 
     def write_own(k, carry):
-        column, value = rates(k, row_rate[k])
+        column, value = rates(k, row_rate[k], width + k, base + k)
         for c in range(5):
             own_out[pl.ds(c * width + column, 1), :] = value[c : c + 1]
         return carry
 
     def write_upper(k, carry):
-        column, value = rates(k, None)
+        column, value = rates(up + k, None, 2 * width + k, upper_base + k)
         for c in range(5):
             next_out[pl.ds(c * width + column, 1), :] = value[c : c + 1]
         return carry
 
     lax.fori_loop(0, length + 1, write_own, 0)
-    lax.fori_loop(cap + 1, cap + length + 3, write_upper, 0)
+    lax.fori_loop(0, length + 2, write_upper, 0)
 
 
 def shards(positions, velocity, density, pressure, counts, pair_list):
@@ -873,6 +892,7 @@
     cap = 2 * leaf_sub
     most = cap * CAND
     splits = LEAF // ROWS
+    seats = 2 * upper_seat_of(cap)
 
     own_part, next_part = pl.pallas_call(
         functools.partial(step_kernel, width, sub_count, slots),
@@ -887,10 +907,11 @@
         ]
         + [pltpu.SMEM((most * splits + 2,), jnp.int32)] * 3
         + [
-            pltpu.VMEM((4 * width + 1, 8, LEAF), F32),
-            pltpu.VMEM((4 * width + 1, 32, LEAF), F32),
-            pltpu.VMEM((2 * cap + 3, 24, LEAF), F32),
-            pltpu.VMEM((2 * cap + 3, 64, LEAF), F32),
+            pltpu.SMEM((4 * width,), jnp.int32),
+            pltpu.VMEM(((4 * width + 1) * 8, LEAF), F32),
+            pltpu.VMEM(((4 * width + 1) * 32, LEAF), F32),
+            pltpu.VMEM((seats * 24, LEAF), F32),
+            pltpu.VMEM((seats * 64, LEAF), F32),
             pltpu.VMEM((cap * splits, 6 * ROWS, LEAF), BF16),
             pltpu.VMEM((cap * splits, ROWS, LEAF), BF16),
             pltpu.VMEM((cap * splits, 3 * ROWS, LEAF), BF16),
@@ -906,7 +927,7 @@
             pltpu.VMEM((3 * ROWS, LEAF), F32),
             pltpu.VMEM((ROWS, LEAF), F32),
             pltpu.VMEM((4 * ROWS, LEAF), F32),
-            pltpu.VMEM((2 * cap + 3, 40, LEAF), F32),
+            pltpu.VMEM((seats, 40, LEAF), F32),
             pltpu.VMEM((cap * splits, 5, ROWS, LEAF), F32),
             pltpu.VMEM((cap + 1, 8, LEAF), F32),
         ],

time: 63.6 us -> 68.7 us (1.080)
  waiting for transfers between devices: 16 us -> 20.2 us
  Pallas kernels: 27.7 us -> 29.1 us
    ppermute x6, waiting for transfers between devices: 5.41 us -> 11.4 us  [shifted(): lax.ppermute(shard, axis, [(i, (i + by) % peers) for i in range(peers)])]
    ppermute x6, starting transfers between devices: 9.03 us -> 6.35 us  [shifted(): lax.ppermute(shard, axis, [(i, (i + by) % peers) for i in range(peers)])]
    ppermute x4, starting transfers between devices: 9.67 us -> 11.9 us  [swapped(): return lax.ppermute(shard, axis, [(i, i ^ mask) for i in range(peers)])]
    ppermute x4, waiting for transfers between devices: 10.6 us -> 8.72 us  [swapped(): return lax.ppermute(shard, axis, [(i, i ^ mask) for i in range(peers)])]
    pallas_call x1, Pallas kernels: 25.8 us -> 27.3 us  [shards(): pl.pallas_call(functools.partial(step_kernel, width, sub_count, slots), o...]
  transfers between devices with their start and end apart: 10 -> 10, of which waited for: 8 -> 8; matrix products, arithmetic and copies ran while one was open for 2% -> 1% of each run, Pallas kernels for 0% -> 0%
where the time goes in v2:
time: 68.7 us; the launch traced here: 69.4 us
  Pallas kernels  29.1 us (42%)
  waiting for transfers between devices  20.2 us (29%)
  starting transfers between devices  18.3 us (27%)
  other arithmetic  1.04 us (2%)
    pallas_call x1, Pallas kernels, shards(): pl.pallas_call(functools.partial(step_kernel, width, sub_count, slots), o...  27.3 us
    ppermute x4, starting transfers between devices, swapped(): return lax.ppermute(shard, axis, [(i, i ^ mask) for i in range(peers)])  11.9 us
    ppermute x6, waiting for transfers between devices, shifted(): lax.ppermute(shard, axis, [(i, (i + by) % peers) for i in range(peers)])  11.4 us
    ppermute x4, waiting for transfers between devices, swapped(): return lax.ppermute(shard, axis, [(i, i ^ mask) for i in range(peers)])  8.72 us
    ppermute x6, starting transfers between devices, shifted(): lax.ppermute(shard, axis, [(i, (i + by) % peers) for i in range(peers)])  6.35 us
    pallas_call x1, Pallas kernels, shards(): pl.pallas_call(functools.partial(pack_kernel, width, leaf_sub), out_shape...  1.88 us
  transfers between devices with their start and end apart: 10, of which 8 were waited for; matrix products, arithmetic and copies ran while one was open for 1% of the time, Pallas kernels for 0%

profile of v2, /device:TPU:0, one launch (start us, length us, event | category | flops | bytes accessed | tf_op | source)
XLA Modules:
  0.0 69.4 jit_solution(17082636709554253781)
XLA Ops:
  0.0 1.9 %pack.1 = (f32[8,4096]{1,0:T(8,128)}, f32[4,128]{1,0:T(4,128)}) custom-call(s32[32]{0:T(128)} %counts.1, s32[1,32]{1,0:T(1,128)} %bitcast.13, f32[3,4096]{1,0:T(4,128)} %positions.1, f32[3,4096]{1,0:T(4,128)} %velocity.1, f32[1,4096]{1,0:T(1,128)} %bitcast.10, f32[1,4096]{1,0:T(1,128)} %bitcast.11, s32[3,40]{1,0:T(4,128)} %pair_list.1), custom_call_target="tpu_custom_call" | custom-call | tf_op jit(solution)/shard_map/pack/pallas_call | solution.py:862
  1.9 3.3 %collective-permute-start.1 = (f32[4,128]{1,0:T(4,128)}, f32[4,128]{1,0:T(4,128)S(1)}, u32[]{:S(2)}, u32[]{:S(2)}) collective-permute-start(f32[4,128]{1,0:T(4,128)} %get-tuple-element.11), channel_id=1, source_target_pairs={{0,28},{4,0},{8,4},{12,8},{16,12},{20,16},{24,20},{28,24},{1,29},{... | collective-permute-start | bytes 6152 | tf_op jit(solution)/shard_map/ppermute | solution.py:30
  5.2 0.0 collective-permute-start
  5.2 0.0 copy-start.1
  5.2 0.0 copy-start
  5.2 1.0 %compare_select_fusion.own_ref = f32[8,4096]{1,0:T(8,128)S(1)} fusion(f32[8,4096]{1,0:T(8,128)} %get-tuple-element.12), kind=kLoop, calls=%fused_computation | loop fusion | flops 65536 | bytes 262144 | tf_op jit(solution)/shard_map/jit(_where)/select_n | solution.py:881
  6.2 0.0 copy-done.1
  6.2 0.5 collective-permute-done.1
  6.7 2.6 %collective-permute-done = f32[4,128]{1,0:T(4,128)S(1)} collective-permute-done((f32[4,128]{1,0:T(4,128)}, f32[4,128]{1,0:T(4,128)S(1)}, u32[]{:S(2)}, u32[]{:S(2)}) %collective-permute-start) | collective-permute-done | bytes 2080 | tf_op jit(solution)/shard_map/ppermute | solution.py:30
  9.3 1.6 %collective-permute-start.2 = (f32[1,3,4,128]{3,2,1,0:T(4,128)S(1)}, f32[1,3,4,128]{3,2,1,0:T(4,128)S(1)}, u32[]{:S(2)}, u32[]{:S(2)}) collective-permute-start(f32[1,3,4,128]{3,2,1,0:T(4,128)S(1)} %maximum_bitcast_fusion), channel_id=1, source_target_pairs={{0,1},{1,0},{2,3},{3,2},{4,5},{5,4},{6,7},{7,6},{8,9},{9,8},{10,11... | collective-permute-start | bytes 18440 | tf_op jit(solution)/shard_map/ppermute | solution.py:35
  10.9 0.0 copy-done
  10.9 0.0 collective-permute-start.5
  10.9 0.5 collective-permute-start.4
  11.4 0.0 collective-permute-start.6
  11.4 1.5 %collective-permute-done.2 = f32[1,3,4,128]{3,2,1,0:T(4,128)S(1)} collective-permute-done((f32[1,3,4,128]{3,2,1,0:T(4,128)S(1)}, f32[1,3,4,128]{3,2,1,0:T(4,128)S(1)}, u32[]{:S(2)}, u32[]{:S(2)}) %collective-permute-start.2) | collective-permute-done | bytes 6176 | tf_op jit(solution)/shard_map/ppermute | solution.py:35
  13.0 2.6 %collective-permute-start.3 = (f32[2,3,4,128]{3,2,1,0:T(4,128)S(1)}, f32[2,3,4,128]{3,2,1,0:T(4,128)S(1)}, u32[]{:S(2)}, u32[]{:S(2)}) collective-permute-start(f32[2,3,4,128]{3,2,1,0:T(4,128)S(1)} %pad_maximum_fusion), channel_id=1, source_target_pairs={{0,2},{1,3},{2,0},{3,1},{4,6},{5,7},{6,4},{7,5},{8,10},{9,11},{10,... | collective-permute-start | bytes 36872 | tf_op jit(solution)/shard_map/ppermute | solution.py:35
  15.6 2.0 %collective-permute-done.3 = f32[2,3,4,128]{3,2,1,0:T(4,128)S(1)} collective-permute-done((f32[2,3,4,128]{3,2,1,0:T(4,128)S(1)}, f32[2,3,4,128]{3,2,1,0:T(4,128)S(1)}, u32[]{:S(2)}, u32[]{:S(2)}) %collective-permute-start.3) | collective-permute-done | bytes 12320 | tf_op jit(solution)/shard_map/ppermute | solution.py:35
  17.6 0.0 collective-permute-done.5.upper_ref
  17.6 0.0 collective-permute-done.4.lower_ref
  17.6 0.2 collective-permute-done.6.beyond_ref
  17.8 27.3 %hydro_step.1 = (f32[160,128]{1,0:T(8,128)S(1)}, f32[160,128]{1,0:T(8,128)S(1)}) custom-call(s32[6144]{0:T(1024)S(1)} %bitcast.9, f32[8,4096]{1,0:T(8,128)S(1)} %collective-permute-done.4.lower_ref, f32[8,4096]{1,0:T(8,128)S(1)} %compare_select_fusion.own_ref, f32[8,4096]{1,0:T(8,128)S(1)} %collective-permute-done.5.upper_ref, ...), custom_call_target="tpu_custom_call" | custom-call | tf_op jit(solution)/shard_map/hydro_step/pallas_call | solution.py:897
  45.1 2.5 %collective-permute-start.7 = (f32[160,128]{1,0:T(8,128)S(1)}, f32[160,128]{1,0:T(8,128)S(1)}, u32[]{:S(2)}, u32[]{:S(2)}) collective-permute-start(f32[160,128]{1,0:T(8,128)S(1)} %get-tuple-element.16), channel_id=1, source_target_pairs={{0,4},{4,8},{8,12},{12,16},{16,20},{20,24},{24,28},{28,0},{1,5},{5... | collective-permute-start | bytes 245768 | tf_op jit(solution)/shard_map/ppermute | solution.py:30
  47.6 8.1 %collective-permute-done.7 = f32[160,128]{1,0:T(8,128)S(1)} collective-permute-done((f32[160,128]{1,0:T(8,128)S(1)}, f32[160,128]{1,0:T(8,128)S(1)}, u32[]{:S(2)}, u32[]{:S(2)}) %collective-permute-start.7) | collective-permute-done | bytes 81952 | tf_op jit(solution)/shard_map/ppermute | solution.py:30
  55.7 1.7 %collective-permute-start.8 = (f32[160,128]{1,0:T(8,128)S(1)}, f32[160,128]{1,0:T(8,128)S(1)}, u32[]{:S(2)}, u32[]{:S(2)}) collective-permute-start(f32[160,128]{1,0:T(8,128)S(1)} %add.9), channel_id=1, source_target_pairs={{0,1},{1,0},{2,3},{3,2},{4,5},{5,4},{6,7},{7,6},{8,9},{9,8},{10,11... | collective-permute-start | bytes 245768 | tf_op jit(solution)/shard_map/ppermute | solution.py:35
  57.5 2.8 %collective-permute-done.8 = f32[160,128]{1,0:T(8,128)S(1)} collective-permute-done((f32[160,128]{1,0:T(8,128)S(1)}, f32[160,128]{1,0:T(8,128)S(1)}, u32[]{:S(2)}, u32[]{:S(2)}) %collective-permute-start.8) | collective-permute-done | bytes 81952 | tf_op jit(solution)/shard_map/ppermute | solution.py:35
  60.3 6.0 %collective-permute-start.9 = (f32[160,128]{1,0:T(8,128)S(1)}, f32[160,128]{1,0:T(8,128)S(1)}, u32[]{:S(2)}, u32[]{:S(2)}) collective-permute-start(f32[160,128]{1,0:T(8,128)S(1)} %add.10), channel_id=1, source_target_pairs={{0,2},{1,3},{2,0},{3,1},{4,6},{5,7},{6,4},{7,5},{8,10},{9,11},{10,... | collective-permute-start | bytes 245768 | tf_op jit(solution)/shard_map/ppermute | solution.py:35
  66.3 2.4 %collective-permute-done.9 = f32[160,128]{1,0:T(8,128)S(1)} collective-permute-done((f32[160,128]{1,0:T(8,128)S(1)}, f32[160,128]{1,0:T(8,128)S(1)}, u32[]{:S(2)}, u32[]{:S(2)}) %collective-permute-start.9) | collective-permute-done | bytes 81952 | tf_op jit(solution)/shard_map/ppermute | solution.py:35
  68.7 0.7 reshape.6
  (7 shorter events, 0.1 us)
Async XLA Ops:
  1.9 4.9 %collective-permute-start.1 = (f32[4,128]{1,0:T(4,128)}, f32[4,128]{1,0:T(4,128)S(1)}, u32[]{:S(2)}, u32[]{:S(2)}) collective-permute-start(f32[4,128]{1,0:T(4,128)} %get-tuple-element.11), channel_id=1, source_target_pairs={{0,28},{4,0},{8,4},{12,8},{16,12},{20,16},{24,20},{28,24},{1,29},{... | collective-permute-start | bytes 6152 | tf_op jit(solution)/shard_map/ppermute | solution.py:30
  5.2 4.1 %collective-permute-start = (f32[4,128]{1,0:T(4,128)}, f32[4,128]{1,0:T(4,128)S(1)}, u32[]{:S(2)}, u32[]{:S(2)}) collective-permute-start(f32[4,128]{1,0:T(4,128)} %get-tuple-element.11), channel_id=1, source_target_pairs={{0,4},{4,8},{8,12},{12,16},{16,20},{20,24},{24,28},{28,0},{1,5},{5... | collective-permute-start | bytes 6152 | tf_op jit(solution)/shard_map/ppermute | solution.py:30
  5.2 1.0 %copy-start.1 = (f32[4,128]{1,0:T(4,128)S(1)}, f32[4,128]{1,0:T(4,128)}, u32[]{:S(2)}) copy-start(f32[4,128]{1,0:T(4,128)} %get-tuple-element.11) | copy-start | bytes 6148
  5.2 5.7 %copy-start = (f32[8,4096]{1,0:T(8,128)S(1)}, f32[8,4096]{1,0:T(8,128)}, u32[]{:S(2)}) copy-start(f32[8,4096]{1,0:T(8,128)} %get-tuple-element.12) | copy-start | bytes 393220
  9.3 3.6 %collective-permute-start.2 = (f32[1,3,4,128]{3,2,1,0:T(4,128)S(1)}, f32[1,3,4,128]{3,2,1,0:T(4,128)S(1)}, u32[]{:S(2)}, u32[]{:S(2)}) collective-permute-start(f32[1,3,4,128]{3,2,1,0:T(4,128)S(1)} %maximum_bitcast_fusion), channel_id=1, source_target_pairs={{0,1},{1,0},{2,3},{3,2},{4,5},{5,4},{6,7},{7,6},{8,9},{9,8},{10,11... | collective-permute-start | bytes 18440 | tf_op jit(solution)/shard_map/ppermute | solution.py:35
  10.9 6.7 %collective-permute-start.5 = (f32[8,4096]{1,0:T(8,128)S(1)}, f32[8,4096]{1,0:T(8,128)S(1)}, u32[]{:S(2)}, u32[]{:S(2)}) collective-permute-start(f32[8,4096]{1,0:T(8,128)S(1)} %copy-done), channel_id=1, source_target_pairs={{0,28},{4,0},{8,4},{12,8},{16,12},{20,16},{24,20},{28,24},{1,29},{... | collective-permute-start | bytes 393224 | tf_op jit(solution)/shard_map/ppermute | solution.py:30
  10.9 6.7 %collective-permute-start.4 = (f32[8,4096]{1,0:T(8,128)S(1)}, f32[8,4096]{1,0:T(8,128)S(1)}, u32[]{:S(2)}, u32[]{:S(2)}) collective-permute-start(f32[8,4096]{1,0:T(8,128)S(1)} %copy-done), channel_id=1, source_target_pairs={{0,4},{4,8},{8,12},{12,16},{16,20},{20,24},{24,28},{28,0},{1,5},{5... | collective-permute-start | bytes 393224 | tf_op jit(solution)/shard_map/ppermute | solution.py:30
  11.4 6.4 %collective-permute-start.6 = (f32[8,4096]{1,0:T(8,128)S(1)}, f32[8,4096]{1,0:T(8,128)S(1)}, u32[]{:S(2)}, u32[]{:S(2)}) collective-permute-start(f32[8,4096]{1,0:T(8,128)S(1)} %copy-done), channel_id=1, source_target_pairs={{0,24},{4,28},{8,0},{12,4},{16,8},{20,12},{24,16},{28,20},{1,25},{... | collective-permute-start | bytes 393224 | tf_op jit(solution)/shard_map/ppermute | solution.py:30
  13.0 4.6 %collective-permute-start.3 = (f32[2,3,4,128]{3,2,1,0:T(4,128)S(1)}, f32[2,3,4,128]{3,2,1,0:T(4,128)S(1)}, u32[]{:S(2)}, u32[]{:S(2)}) collective-permute-start(f32[2,3,4,128]{3,2,1,0:T(4,128)S(1)} %pad_maximum_fusion), channel_id=1, source_target_pairs={{0,2},{1,3},{2,0},{3,1},{4,6},{5,7},{6,4},{7,5},{8,10},{9,11},{10,... | collective-permute-start | bytes 36872 | tf_op jit(solution)/shard_map/ppermute | solution.py:35
  45.1 10.6 %collective-permute-start.7 = (f32[160,128]{1,0:T(8,128)S(1)}, f32[160,128]{1,0:T(8,128)S(1)}, u32[]{:S(2)}, u32[]{:S(2)}) collective-permute-start(f32[160,128]{1,0:T(8,128)S(1)} %get-tuple-element.16), channel_id=1, source_target_pairs={{0,4},{4,8},{8,12},{12,16},{16,20},{20,24},{24,28},{28,0},{1,5},{5... | collective-permute-start | bytes 245768 | tf_op jit(solution)/shard_map/ppermute | solution.py:30
  55.7 4.5 %collective-permute-start.8 = (f32[160,128]{1,0:T(8,128)S(1)}, f32[160,128]{1,0:T(8,128)S(1)}, u32[]{:S(2)}, u32[]{:S(2)}) collective-permute-start(f32[160,128]{1,0:T(8,128)S(1)} %add.9), channel_id=1, source_target_pairs={{0,1},{1,0},{2,3},{3,2},{4,5},{5,4},{6,7},{7,6},{8,9},{9,8},{10,11... | collective-permute-start | bytes 245768 | tf_op jit(solution)/shard_map/ppermute | solution.py:35
  60.3 8.5 %collective-permute-start.9 = (f32[160,128]{1,0:T(8,128)S(1)}, f32[160,128]{1,0:T(8,128)S(1)}, u32[]{:S(2)}, u32[]{:S(2)}) collective-permute-start(f32[160,128]{1,0:T(8,128)S(1)} %add.10), channel_id=1, source_target_pairs={{0,2},{1,3},{2,0},{3,1},{4,6},{5,7},{6,4},{7,5},{8,10},{9,11},{10,... | collective-permute-start | bytes 245768 | tf_op jit(solution)/shard_map/ppermute | solution.py:35

commit v3 on v2

--- a/solution.py
+++ b/solution.py
@@ -17,7 +17,7 @@
 MOMENT_REG = 0.05
 AREA_FLOOR = 0.0001
 AWAY = 64.0
-UNROLL = 8
+UNROLL = 12
 ROWS = 64
 ROWS_LOG = 6
 COST_LEAF, COST_SLOT, COST_PART = 17, 3, 5
@@ -380,7 +380,7 @@
 ):
     whole = 4 * width
     leaf_sub = width // sub_count
-    cap = 2 * leaf_sub
+    cap = -(-2 * leaf_sub // 4) * 4
     up = upper_seat_of(cap)
     stride = rec.shape[0] // (12 * sub_count)
     block = 4 * stride
@@ -687,12 +687,12 @@
             for k in range(5):
                 near_plane[place, k] = planes[rows, k * LEAF : (k + 1) * LEAF]
 
-    def turn_two(pair, carry):
-        turn_home(2 * pair)
-        turn_home(2 * pair + 1)
-        return carry
-
-    lax.fori_loop(0, (length + 1) // 2, turn_two, 0)
+    def turn_four(group, carry):
+        for k in range(4):
+            turn_home(4 * group + k)
+        return carry
+
+    lax.fori_loop(0, (length + 3) // 4, turn_four, 0)
 
     def prepare_slot(index, count):
         slot = mine[index]
@@ -736,11 +736,14 @@
         far_half[index, 0:5] = jnp.concatenate([0.5 * far[3:6], far[6:8]], axis=0)
         return count
 
-    def prepare_two(pair, count):
-        return prepare_slot(2 * pair + 1, prepare_slot(2 * pair, count))
-
-    mine[kept] = mine[0]
-    item_count = lax.fori_loop(0, (kept + 1) // 2, prepare_two, 0)
+    def prepare_four(group, count):
+        for k in range(4):
+            count = prepare_slot(4 * group + k, count)
+        return count
+
+    for extra in range(3):
+        mine[kept + extra] = mine[0]
+    item_count = lax.fori_loop(0, (kept + 3) // 4, prepare_four, 0)
     for extra in range(2):
         item_left[item_count + extra] = 0
         item_index[item_count + extra] = 0
@@ -889,7 +892,7 @@
         lists = jnp.concatenate([lists, swapped(lists, "sub", mask)], axis=0)
         mask *= 2
     rec = lists.astype(jnp.int32).reshape(-1)
-    cap = 2 * leaf_sub
+    cap = -(-2 * leaf_sub // 4) * 4
     most = cap * CAND
     splits = LEAF // ROWS
     seats = 2 * upper_seat_of(cap)
@@ -901,7 +904,7 @@
         out_specs=[vmem, vmem],
         scratch_shapes=[
             pltpu.SMEM((3 * sub_count * slots + 2 * UNROLL,), jnp.int32),
-            pltpu.SMEM((most + 1,), jnp.int32),
+            pltpu.SMEM((most + 3,), jnp.int32),
             pltpu.SMEM((7 * width + 1,), jnp.int32),
             pltpu.SMEM((width,), jnp.int32),
         ]

time: 68.7 us -> 68.9 us (level); the launches traced: 69.4 us -> 68.2 us
  Pallas kernels: 29.1 us -> 34.5 us
  starting transfers between devices: 18.3 us -> 13.8 us
  waiting for transfers between devices: 20.2 us -> 18.2 us
    pallas_call x1, Pallas kernels: 27.3 us -> 32.6 us  [shards(): pl.pallas_call(functools.partial(step_kernel, width, sub_count, slots), o...]
    ppermute x6, waiting for transfers between devices: 11.4 us -> 7.5 us  [shifted(): lax.ppermute(shard, axis, [(i, (i + by) % peers) for i in range(peers)])]
    ppermute x4, starting transfers between devices: 11.9 us -> 9.35 us  [swapped(): return lax.ppermute(shard, axis, [(i, i ^ mask) for i in range(peers)])]
    ppermute x4, waiting for transfers between devices: 8.72 us -> 10.6 us  [swapped(): return lax.ppermute(shard, axis, [(i, i ^ mask) for i in range(peers)])]
    ppermute x6, starting transfers between devices: 6.35 us -> 4.48 us  [shifted(): lax.ppermute(shard, axis, [(i, (i + by) % peers) for i in range(peers)])]
where the time goes in v3:
time: 68.9 us; the launch traced here: 68.2 us
  Pallas kernels  34.5 us (50%)
  waiting for transfers between devices  18.2 us (26%)
  starting transfers between devices  13.8 us (20%)
  other arithmetic  1.04 us (2%)
    pallas_call x1, Pallas kernels, shards(): pl.pallas_call(functools.partial(step_kernel, width, sub_count, slots), o...  32.6 us
    ppermute x4, waiting for transfers between devices, swapped(): return lax.ppermute(shard, axis, [(i, i ^ mask) for i in range(peers)])  10.6 us
    ppermute x4, starting transfers between devices, swapped(): return lax.ppermute(shard, axis, [(i, i ^ mask) for i in range(peers)])  9.35 us
    ppermute x6, waiting for transfers between devices, shifted(): lax.ppermute(shard, axis, [(i, (i + by) % peers) for i in range(peers)])  7.5 us
    ppermute x6, starting transfers between devices, shifted(): lax.ppermute(shard, axis, [(i, (i + by) % peers) for i in range(peers)])  4.48 us
    pallas_call x1, Pallas kernels, shards(): pl.pallas_call(functools.partial(pack_kernel, width, leaf_sub), out_shape...  1.88 us
  transfers between devices with their start and end apart: 10, of which 8 were waited for; matrix products, arithmetic and copies ran while one was open for 1% of the time, Pallas kernels for 0%

profile of v3, /device:TPU:0, one launch (start us, length us, event | category | flops | bytes accessed | tf_op | source)
XLA Modules:
  0.0 68.2 jit_solution(85608272645397821)
XLA Ops:
  0.0 1.9 %pack.1 = (f32[8,4096]{1,0:T(8,128)}, f32[4,128]{1,0:T(4,128)}) custom-call(s32[32]{0:T(128)} %counts.1, s32[1,32]{1,0:T(1,128)} %bitcast.13, f32[3,4096]{1,0:T(4,128)} %positions.1, f32[3,4096]{1,0:T(4,128)} %velocity.1, f32[1,4096]{1,0:T(1,128)} %bitcast.10, f32[1,4096]{1,0:T(1,128)} %bitcast.11, s32[3,40]{1,0:T(4,128)} %pair_list.1), custom_call_target="tpu_custom_call" | custom-call | tf_op jit(solution)/shard_map/pack/pallas_call | solution.py:865
  1.9 3.3 %collective-permute-start.1 = (f32[4,128]{1,0:T(4,128)}, f32[4,128]{1,0:T(4,128)S(1)}, u32[]{:S(2)}, u32[]{:S(2)}) collective-permute-start(f32[4,128]{1,0:T(4,128)} %get-tuple-element.11), channel_id=1, source_target_pairs={{0,28},{4,0},{8,4},{12,8},{16,12},{20,16},{24,20},{28,24},{1,29},{... | collective-permute-start | bytes 6152 | tf_op jit(solution)/shard_map/ppermute | solution.py:30
  5.2 0.0 collective-permute-start
  5.2 0.0 copy-start.1
  5.2 0.0 copy-start
  5.2 1.0 %compare_select_fusion.own_ref = f32[8,4096]{1,0:T(8,128)S(1)} fusion(f32[8,4096]{1,0:T(8,128)} %get-tuple-element.12), kind=kLoop, calls=%fused_computation | loop fusion | flops 65536 | bytes 262144 | tf_op jit(solution)/shard_map/jit(_where)/select_n | solution.py:884
  6.2 0.0 copy-done.1
  6.2 0.5 collective-permute-done.1
  6.7 2.6 %collective-permute-done = f32[4,128]{1,0:T(4,128)S(1)} collective-permute-done((f32[4,128]{1,0:T(4,128)}, f32[4,128]{1,0:T(4,128)S(1)}, u32[]{:S(2)}, u32[]{:S(2)}) %collective-permute-start) | collective-permute-done | bytes 2080 | tf_op jit(solution)/shard_map/ppermute | solution.py:30
  9.3 1.6 %collective-permute-start.2 = (f32[1,3,4,128]{3,2,1,0:T(4,128)S(1)}, f32[1,3,4,128]{3,2,1,0:T(4,128)S(1)}, u32[]{:S(2)}, u32[]{:S(2)}) collective-permute-start(f32[1,3,4,128]{3,2,1,0:T(4,128)S(1)} %maximum_bitcast_fusion), channel_id=1, source_target_pairs={{0,1},{1,0},{2,3},{3,2},{4,5},{5,4},{6,7},{7,6},{8,9},{9,8},{10,11... | collective-permute-start | bytes 18440 | tf_op jit(solution)/shard_map/ppermute | solution.py:35
  10.9 0.0 copy-done
  10.9 0.0 collective-permute-start.5
  10.9 0.5 collective-permute-start.4
  11.4 0.0 collective-permute-start.6
  11.4 1.5 %collective-permute-done.2 = f32[1,3,4,128]{3,2,1,0:T(4,128)S(1)} collective-permute-done((f32[1,3,4,128]{3,2,1,0:T(4,128)S(1)}, f32[1,3,4,128]{3,2,1,0:T(4,128)S(1)}, u32[]{:S(2)}, u32[]{:S(2)}) %collective-permute-start.2) | collective-permute-done | bytes 6176 | tf_op jit(solution)/shard_map/ppermute | solution.py:35
  13.0 2.6 %collective-permute-start.3 = (f32[2,3,4,128]{3,2,1,0:T(4,128)S(1)}, f32[2,3,4,128]{3,2,1,0:T(4,128)S(1)}, u32[]{:S(2)}, u32[]{:S(2)}) collective-permute-start(f32[2,3,4,128]{3,2,1,0:T(4,128)S(1)} %pad_maximum_fusion), channel_id=1, source_target_pairs={{0,2},{1,3},{2,0},{3,1},{4,6},{5,7},{6,4},{7,5},{8,10},{9,11},{10,... | collective-permute-start | bytes 36872 | tf_op jit(solution)/shard_map/ppermute | solution.py:35
  15.6 2.0 %collective-permute-done.3 = f32[2,3,4,128]{3,2,1,0:T(4,128)S(1)} collective-permute-done((f32[2,3,4,128]{3,2,1,0:T(4,128)S(1)}, f32[2,3,4,128]{3,2,1,0:T(4,128)S(1)}, u32[]{:S(2)}, u32[]{:S(2)}) %collective-permute-start.3) | collective-permute-done | bytes 12320 | tf_op jit(solution)/shard_map/ppermute | solution.py:35
  17.6 0.0 collective-permute-done.5.upper_ref
  17.6 0.0 collective-permute-done.4.lower_ref
  17.6 0.2 collective-permute-done.6.beyond_ref
  17.8 32.6 %hydro_step.1 = (f32[160,128]{1,0:T(8,128)S(1)}, f32[160,128]{1,0:T(8,128)S(1)}) custom-call(s32[6144]{0:T(1024)S(1)} %bitcast.9, f32[8,4096]{1,0:T(8,128)S(1)} %collective-permute-done.4.lower_ref, f32[8,4096]{1,0:T(8,128)S(1)} %compare_select_fusion.own_ref, f32[8,4096]{1,0:T(8,128)S(1)} %collective-permute-done.5.upper_ref, ...), custom_call_target="tpu_custom_call" | custom-call | tf_op jit(solution)/shard_map/hydro_step/pallas_call | solution.py:900
  50.4 0.6 collective-permute-start.7
  51.0 4.2 %collective-permute-done.7 = f32[160,128]{1,0:T(8,128)S(1)} collective-permute-done((f32[160,128]{1,0:T(8,128)S(1)}, f32[160,128]{1,0:T(8,128)S(1)}, u32[]{:S(2)}, u32[]{:S(2)}) %collective-permute-start.7) | collective-permute-done | bytes 81952 | tf_op jit(solution)/shard_map/ppermute | solution.py:30
  55.2 0.7 %collective-permute-start.8 = (f32[160,128]{1,0:T(8,128)S(1)}, f32[160,128]{1,0:T(8,128)S(1)}, u32[]{:S(2)}, u32[]{:S(2)}) collective-permute-start(f32[160,128]{1,0:T(8,128)S(1)} %add.9), channel_id=1, source_target_pairs={{0,1},{1,0},{2,3},{3,2},{4,5},{5,4},{6,7},{7,6},{8,9},{9,8},{10,11... | collective-permute-start | bytes 245768 | tf_op jit(solution)/shard_map/ppermute | solution.py:35
  55.9 3.8 %collective-permute-done.8 = f32[160,128]{1,0:T(8,128)S(1)} collective-permute-done((f32[160,128]{1,0:T(8,128)S(1)}, f32[160,128]{1,0:T(8,128)S(1)}, u32[]{:S(2)}, u32[]{:S(2)}) %collective-permute-start.8) | collective-permute-done | bytes 81952 | tf_op jit(solution)/shard_map/ppermute | solution.py:35
  59.7 4.5 %collective-permute-start.9 = (f32[160,128]{1,0:T(8,128)S(1)}, f32[160,128]{1,0:T(8,128)S(1)}, u32[]{:S(2)}, u32[]{:S(2)}) collective-permute-start(f32[160,128]{1,0:T(8,128)S(1)} %add.10), channel_id=1, source_target_pairs={{0,2},{1,3},{2,0},{3,1},{4,6},{5,7},{6,4},{7,5},{8,10},{9,11},{10,... | collective-permute-start | bytes 245768 | tf_op jit(solution)/shard_map/ppermute | solution.py:35
  64.2 3.3 %collective-permute-done.9 = f32[160,128]{1,0:T(8,128)S(1)} collective-permute-done((f32[160,128]{1,0:T(8,128)S(1)}, f32[160,128]{1,0:T(8,128)S(1)}, u32[]{:S(2)}, u32[]{:S(2)}) %collective-permute-start.9) | collective-permute-done | bytes 81952 | tf_op jit(solution)/shard_map/ppermute | solution.py:35
  67.6 0.7 reshape.6
  (7 shorter events, 0.1 us)
Async XLA Ops:
  1.9 4.9 %collective-permute-start.1 = (f32[4,128]{1,0:T(4,128)}, f32[4,128]{1,0:T(4,128)S(1)}, u32[]{:S(2)}, u32[]{:S(2)}) collective-permute-start(f32[4,128]{1,0:T(4,128)} %get-tuple-element.11), channel_id=1, source_target_pairs={{0,28},{4,0},{8,4},{12,8},{16,12},{20,16},{24,20},{28,24},{1,29},{... | collective-permute-start | bytes 6152 | tf_op jit(solution)/shard_map/ppermute | solution.py:30
  5.2 4.1 %collective-permute-start = (f32[4,128]{1,0:T(4,128)}, f32[4,128]{1,0:T(4,128)S(1)}, u32[]{:S(2)}, u32[]{:S(2)}) collective-permute-start(f32[4,128]{1,0:T(4,128)} %get-tuple-element.11), channel_id=1, source_target_pairs={{0,4},{4,8},{8,12},{12,16},{16,20},{20,24},{24,28},{28,0},{1,5},{5... | collective-permute-start | bytes 6152 | tf_op jit(solution)/shard_map/ppermute | solution.py:30
  5.2 1.0 %copy-start.1 = (f32[4,128]{1,0:T(4,128)S(1)}, f32[4,128]{1,0:T(4,128)}, u32[]{:S(2)}) copy-start(f32[4,128]{1,0:T(4,128)} %get-tuple-element.11) | copy-start | bytes 6148
  5.2 5.7 %copy-start = (f32[8,4096]{1,0:T(8,128)S(1)}, f32[8,4096]{1,0:T(8,128)}, u32[]{:S(2)}) copy-start(f32[8,4096]{1,0:T(8,128)} %get-tuple-element.12) | copy-start | bytes 393220
  9.3 3.6 %collective-permute-start.2 = (f32[1,3,4,128]{3,2,1,0:T(4,128)S(1)}, f32[1,3,4,128]{3,2,1,0:T(4,128)S(1)}, u32[]{:S(2)}, u32[]{:S(2)}) collective-permute-start(f32[1,3,4,128]{3,2,1,0:T(4,128)S(1)} %maximum_bitcast_fusion), channel_id=1, source_target_pairs={{0,1},{1,0},{2,3},{3,2},{4,5},{5,4},{6,7},{7,6},{8,9},{9,8},{10,11... | collective-permute-start | bytes 18440 | tf_op jit(solution)/shard_map/ppermute | solution.py:35
  10.9 6.7 %collective-permute-start.5 = (f32[8,4096]{1,0:T(8,128)S(1)}, f32[8,4096]{1,0:T(8,128)S(1)}, u32[]{:S(2)}, u32[]{:S(2)}) collective-permute-start(f32[8,4096]{1,0:T(8,128)S(1)} %copy-done), channel_id=1, source_target_pairs={{0,28},{4,0},{8,4},{12,8},{16,12},{20,16},{24,20},{28,24},{1,29},{... | collective-permute-start | bytes 393224 | tf_op jit(solution)/shard_map/ppermute | solution.py:30
  10.9 6.7 %collective-permute-start.4 = (f32[8,4096]{1,0:T(8,128)S(1)}, f32[8,4096]{1,0:T(8,128)S(1)}, u32[]{:S(2)}, u32[]{:S(2)}) collective-permute-start(f32[8,4096]{1,0:T(8,128)S(1)} %copy-done), channel_id=1, source_target_pairs={{0,4},{4,8},{8,12},{12,16},{16,20},{20,24},{24,28},{28,0},{1,5},{5... | collective-permute-start | bytes 393224 | tf_op jit(solution)/shard_map/ppermute | solution.py:30
  11.4 6.4 %collective-permute-start.6 = (f32[8,4096]{1,0:T(8,128)S(1)}, f32[8,4096]{1,0:T(8,128)S(1)}, u32[]{:S(2)}, u32[]{:S(2)}) collective-permute-start(f32[8,4096]{1,0:T(8,128)S(1)} %copy-done), channel_id=1, source_target_pairs={{0,24},{4,28},{8,0},{12,4},{16,8},{20,12},{24,16},{28,20},{1,25},{... | collective-permute-start | bytes 393224 | tf_op jit(solution)/shard_map/ppermute | solution.py:30
  13.0 4.6 %collective-permute-start.3 = (f32[2,3,4,128]{3,2,1,0:T(4,128)S(1)}, f32[2,3,4,128]{3,2,1,0:T(4,128)S(1)}, u32[]{:S(2)}, u32[]{:S(2)}) collective-permute-start(f32[2,3,4,128]{3,2,1,0:T(4,128)S(1)} %pad_maximum_fusion), channel_id=1, source_target_pairs={{0,2},{1,3},{2,0},{3,1},{4,6},{5,7},{6,4},{7,5},{8,10},{9,11},{10,... | collective-permute-start | bytes 36872 | tf_op jit(solution)/shard_map/ppermute | solution.py:35
  50.4 4.8 %collective-permute-start.7 = (f32[160,128]{1,0:T(8,128)S(1)}, f32[160,128]{1,0:T(8,128)S(1)}, u32[]{:S(2)}, u32[]{:S(2)}) collective-permute-start(f32[160,128]{1,0:T(8,128)S(1)} %get-tuple-element.16), channel_id=1, source_target_pairs={{0,4},{4,8},{8,12},{12,16},{16,20},{20,24},{24,28},{28,0},{1,5},{5... | collective-permute-start | bytes 245768 | tf_op jit(solution)/shard_map/ppermute | solution.py:30
  55.2 4.5 %collective-permute-start.8 = (f32[160,128]{1,0:T(8,128)S(1)}, f32[160,128]{1,0:T(8,128)S(1)}, u32[]{:S(2)}, u32[]{:S(2)}) collective-permute-start(f32[160,128]{1,0:T(8,128)S(1)} %add.9), channel_id=1, source_target_pairs={{0,1},{1,0},{2,3},{3,2},{4,5},{5,4},{6,7},{7,6},{8,9},{9,8},{10,11... | collective-permute-start | bytes 245768 | tf_op jit(solution)/shard_map/ppermute | solution.py:35
  59.7 7.8 %collective-permute-start.9 = (f32[160,128]{1,0:T(8,128)S(1)}, f32[160,128]{1,0:T(8,128)S(1)}, u32[]{:S(2)}, u32[]{:S(2)}) collective-permute-start(f32[160,128]{1,0:T(8,128)S(1)} %add.10), channel_id=1, source_target_pairs={{0,2},{1,3},{2,0},{3,1},{4,6},{5,7},{6,4},{7,5},{8,10},{9,11},{10,... | collective-permute-start | bytes 245768 | tf_op jit(solution)/shard_map/ppermute | solution.py:35
